TPU v7x, 32 devices: a whole 2x2x4 slice. The times are simulated.
32 devices in a mesh: tile: 16 (over z, y, core), seg: 2 (over x).
Axes of the slice: x: 2, y: 2, z: 4, core: 2. Of those that a mesh axis runs over, the one named last changes fastest.
Arguments:
- right_sides: float32 [65536, 512], P(('tile', 'seg')), may hold values from -6 to 6
- leaf_proj: float32 [16, 32, 64, 128], P('tile', 'seg'), may hold values from -0.5 to 0.5
- col_levels: float32 [16, 4, 16, 128, 128], P('tile', None, 'seg'), may hold values from -0.5 to 0.5
- middle_factor: float32 [16, 32, 64, 64], P('tile', 'seg'), may hold values from -0.75 to 0.75
- row_levels: float32 [16, 4, 16, 128, 128], P('tile', None, 'seg'), may hold values from -0.5 to 0.5
- leaf_expand: float32 [16, 32, 128, 64], P('tile', 'seg'), may hold values from -0.1875 to 0.1875
Outputs:
- product: float32 [4096, 512], P(('seg', 'tile'))
All inputs are finite; a program needn't handle non-finite values.
Results may differ from a plain program's by a relative error of at most 0.0001.
Values sent between devices are 32-bit elements; how exact they have to be, the bound alone decides.
No kernel may reach another device: no remote copies, remote signals or barrier semaphores. Data moves between devices by JAX's collectives and lax.ppermute only.
A program may use at most 64 MiB of HBM per device.

v0:
```python
import functools

import jax
import jax.numpy as jnp
from jax import lax
from jax.experimental import pallas as pl
from jax.experimental.pallas import tpu as pltpu
from jax.sharding import PartitionSpec as P

F32 = jnp.float32
BF16 = jnp.bfloat16
CHUNK = 128
ROW = 20_000_000_000


def split(x):
    hi = x.astype(BF16)
    return hi, (x - hi.astype(F32)).astype(BF16)


def dot(a, b, dims=((1,), (0,))):
    return lax.dot_general(a, b, (dims, ((), ())), preferred_element_type=F32)


def wide_of(w):
    return jnp.concatenate(split(w), axis=1)


def product3(wide, v_hi, v_lo):
    depth, width = v_hi.shape
    if width > CHUNK:
        return dot(wide, jnp.concatenate([v_hi, v_hi], axis=0)) + dot(wide[:, :depth], v_lo)
    left = jnp.concatenate([v_hi, v_hi], axis=0)
    right = jnp.concatenate([v_lo, jnp.zeros_like(v_lo)], axis=0)
    both = dot(wide, jnp.concatenate([left, right], axis=1))
    return both[:, :width] + both[:, width:]


def pair_of(hi, lo, first, second, rank, cols=slice(None)):
    return [jnp.concatenate([x[pl.ds(first, rank), cols], x[pl.ds(second, rank), cols]], axis=0) for x in (hi, lo)]


def level_step(level, wide_at, hi, lo, rank, cuts):
    d = 2**level
    for j in range(hi.shape[0] // (2 * rank)):
        first = ((j // d) * 2 * d + j % d) * rank
        second = first + d * rank
        wide = wide_at(j)
        for cols in cuts:
            out_hi, out_lo = split(product3(wide, *pair_of(hi, lo, first, second, rank, cols)))
            for place, half in ((first, 0), (second, 1)):
                hi[pl.ds(place, rank), cols] = out_hi[half * rank:(half + 1) * rank]
                lo[pl.ds(place, rank), cols] = out_lo[half * rank:(half + 1) * rank]


def cuts_of(width):
    odd = width % (2 * CHUNK)
    return ([slice(0, odd)] if odd else []) + [slice(k, k + 2 * CHUNK) for k in range(odd, width, 2 * CHUNK)]


def project(n, wide, x, hi, lo, cuts):
    rank, leaf = wide.shape[0], wide.shape[1] // 2
    for cols in cuts:
        c_hi, c_lo = split(product3(wide, *split(x[n * leaf:(n + 1) * leaf, cols])))
        hi[n * rank:(n + 1) * rank, cols] = c_hi
        lo[n * rank:(n + 1) * rank, cols] = c_lo


def middle(n_seg, mid, outs, hi, lo, cuts):
    box, rank = mid.shape[:2]
    share = box // n_seg
    seg = lax.axis_index("seg")
    for delta in reversed(range(n_seg)):
        base = (seg ^ delta) * share
        for p in range(share):
            wide = wide_of(mid[base + p])
            at = pl.multiple_of((base + p) * rank, rank)
            for cols in cuts:
                out = product3(wide, hi[pl.ds(at, rank), cols], lo[pl.ds(at, rank), cols])
                for k in range(out.shape[1] // CHUNK):
                    target = outs[(cols.start // CHUNK + k) * n_seg + delta]
                    target[p * rank:(p + 1) * rank, :] = out[:, k * CHUNK:(k + 1) * CHUNK]


def column_kernel(n_seg, pieces, start, x_hbm, proj_hbm, col_hbm, mid_hbm, *refs):
    outs, (x_ref, proj_ref, col_ref, mid_ref, hi, lo, sems) = refs[:-7], refs[-7:]
    box, rank, leaf = proj_ref.shape
    levels, pairs = col_ref.shape[:2]
    width = x_ref.shape[1]
    per = box // pieces
    copies = []

    def fetch(src, dst):
        copies.append(pltpu.make_async_copy(src, dst, sems.at[len(copies)]))
        copies[-1].start()
        return copies[-1]

    first = []
    for k in range(pieces):
        rows = pl.ds(k * per * leaf, per * leaf)
        leaves = pl.ds(k * per, per)
        first.append((
            fetch(proj_hbm.at[leaves], proj_ref.at[leaves]),
            fetch(x_hbm.at[rows, pl.ds(start, width)], x_ref.at[rows, :]),
        ))
    halves = [pl.ds(k * (pairs // 2), pairs // 2) for k in range(2)]
    cols = [[fetch(col_hbm.at[k, h], col_ref.at[k, h]) for h in halves] for k in range(levels)]
    mid = fetch(mid_hbm, mid_ref)

    cuts = cuts_of(width)
    for k in range(pieces):
        for copy in first[k]:
            copy.wait()
        for n in range(k * per, (k + 1) * per):
            project(n, wide_of(proj_ref[n]), x_ref, hi, lo, cuts)
    for level in range(levels):
        for copy in cols[level]:
            copy.wait()
        level_step(level, lambda j: wide_of(col_ref[level, j]), hi, lo, rank, cuts)
    mid.wait()
    middle(n_seg, mid_ref, outs, hi, lo, cuts)


def slots_of(n_tile, box, leaf):
    bits = n_tile.bit_length() - 1
    out_rows = box * leaf // n_tile
    relative = [int(format(slot, f"0{bits}b")[::-1], 2) for slot in range(n_tile)]
    return relative, out_rows, min(out_rows, leaf), max(1, out_rows // leaf)


def weights_kernel(row_ref, exp_ref, wide_ref, out_ref):
    out_ref[...] = exp_ref[...]
    for level in range(row_ref.shape[0]):
        for j in range(row_ref.shape[1]):
            wide_ref[level, j] = wide_of(row_ref[level, j])


def expand_weights_kernel(n_tile, exp_ref, other_ref, last_ref):
    box, _, leaf = exp_ref.shape
    tile = lax.axis_index("tile")
    relative, out_rows, unit, pieces = slots_of(n_tile, box, leaf)
    for slot in range(n_tile // 2):
        block = tile ^ relative[slot]
        for piece in range(pieces):
            n = (block * out_rows + piece * unit) // leaf
            both = jnp.concatenate([exp_ref[n], other_ref[n]], axis=0).T
            rows = both[:unit]
            for k in range(1, leaf // unit):
                rows = jnp.where(block % (leaf // unit) == k, both[k * unit:(k + 1) * unit], rows)
            last_ref[slot * pieces + piece] = wide_of(rows)


def row_kernel(n_seg, n_tile, leaf, *refs):
    ins, (row_ref, *outs, hi, lo, full) = refs[:n_seg], refs[n_seg:]
    levels, pairs = row_ref.shape[:2]
    box = 2 * pairs
    rank = hi.shape[0] // box
    share = box // n_seg
    seg = lax.axis_index("seg")
    tile = lax.axis_index("tile")
    for delta in range(n_seg):
        base = (seg ^ delta) * share
        at = pl.multiple_of(base * rank, share * rank)
        v_hi, v_lo = split(ins[delta][...])
        hi[pl.ds(at, share * rank), :] = v_hi
        lo[pl.ds(at, share * rank), :] = v_lo
    for level in range(levels - 1):
        level_step(level, lambda j: row_ref[level, j], hi, lo, rank, [slice(None)])
    for j in range(pairs):
        second = (j + pairs) * rank
        out = product3(row_ref[levels - 1, j], *pair_of(hi, lo, j * rank, second, rank))
        full[j * rank:(j + 1) * rank, :] = out[:rank]
        full[second:second + rank, :] = out[rank:]
    relative, out_rows, unit, pieces = slots_of(n_tile, box, leaf)
    group = n_tile // 4
    for slot in range(n_tile):
        block = tile ^ relative[slot]
        for piece in range(pieces):
            n = (block * out_rows + piece * unit) // leaf
            at = (slot % group * pieces + piece) * rank
            outs[slot // group][at:at + rank, :] = full[pl.ds(pl.multiple_of(n * rank, rank), rank), :]


def expand_kernel(part, own_ref, other_ref, last_ref, out_ref):
    rank = last_ref.shape[2] // 4
    unit = last_ref.shape[1]
    for k in range(own_ref.shape[0] // rank):
        rows = slice(k * rank, (k + 1) * rank)
        v = jnp.concatenate([own_ref[rows, :], other_ref[rows, :]], axis=0)
        wide = last_ref[part * own_ref.shape[0] // rank + k]
        out_ref[k * unit:(k + 1) * unit, :] = product3(wide, *split(v))


def tie(x, *others):
    return lax.optimization_barrier((x, *others))[0]


def shards(n_tile, n_seg, right_sides, leaf_proj, col_levels, middle_factor, row_levels, leaf_expand):
    proj, col, mid, row = leaf_proj[0], col_levels[0], middle_factor[0], row_levels[0]
    expand = jnp.swapaxes(leaf_expand[0], 1, 2)
    box, rank, leaf = proj.shape
    levels, pairs = col.shape[:2]
    chunks = right_sides.shape[1] // CHUNK
    _, out_rows, unit, pieces = slots_of(n_tile, box, leaf)
    bits = n_tile.bit_length() - 1
    part = jax.ShapeDtypeStruct((box * rank // n_seg, CHUNK), F32)
    quarter = jax.ShapeDtypeStruct((n_tile // 4 * pieces * rank, CHUNK), F32)
    summed = jax.ShapeDtypeStruct((box * leaf // 4, CHUNK), F32)
    params = pltpu.CompilerParams(vmem_limit_bytes=16 * 2**20)
    cost = pl.CostEstimate(flops=1_000_000, bytes_accessed=100_000, transcendentals=0)
    in_hbm = pl.BlockSpec(memory_space=pltpu.HBM)
    in_vmem = pl.BlockSpec(memory_space=pltpu.VMEM)

    def column_side(start, count, mid, limit):
        pieces = 4
        width = count * CHUNK
        outs = pl.pallas_call(
            functools.partial(column_kernel, n_seg, pieces, start * CHUNK),
            in_specs=[in_hbm] * 4,
            out_specs=[in_vmem] * (n_seg * count),
            out_shape=[part] * (n_seg * count),
            scratch_shapes=[
                pltpu.VMEM((box * leaf, width), F32),
                pltpu.VMEM(proj.shape, F32),
                pltpu.VMEM(col.shape, F32),
                pltpu.VMEM(mid.shape, F32),
                pltpu.VMEM((box * rank, width), BF16),
                pltpu.VMEM((box * rank, width), BF16),
                pltpu.SemaphoreType.DMA((2 * pieces + 2 * levels + 1,)),
            ],
            compiler_params=pltpu.CompilerParams(vmem_limit_bytes=limit * 2**20),
            cost_estimate=cost,
            name="column_side",
        )(right_sides, proj, col, mid)
        return [outs[k * n_seg:(k + 1) * n_seg] for k in range(count)]

    def row_weights():
        return pl.pallas_call(
            weights_kernel,
            in_specs=[in_vmem] * 2,
            out_specs=[in_vmem] * 2,
            out_shape=[
                jax.ShapeDtypeStruct((levels, pairs, 2 * rank, 4 * rank), BF16),
                jax.ShapeDtypeStruct(expand.shape, F32),
            ],
            compiler_params=params,
            cost_estimate=cost,
            name="row_weights",
        )(row, expand)

    def expand_weights(other):
        return pl.pallas_call(
            functools.partial(expand_weights_kernel, n_tile),
            in_specs=[in_vmem] * 2,
            out_specs=in_vmem,
            out_shape=jax.ShapeDtypeStruct((n_tile // 2 * pieces, unit, 4 * rank), BF16),
            compiler_params=params,
            cost_estimate=cost,
            name="expand_weights",
        )(expand, other)

    def row_side(parts, wide):
        return pl.pallas_call(
            functools.partial(row_kernel, n_seg, n_tile, leaf),
            in_specs=[in_vmem] * (n_seg + 1),
            out_specs=[in_vmem] * 4,
            out_shape=[quarter] * 4,
            scratch_shapes=[pltpu.VMEM((box * rank, CHUNK), t) for t in (BF16, BF16, F32)],
            compiler_params=params,
            cost_estimate=pl.CostEstimate(flops=ROW, bytes_accessed=100_000, transcendentals=0),
            name="row_side",
        )(*parts, wide)

    def expanded(part, own, other, last):
        return pl.pallas_call(
            functools.partial(expand_kernel, part),
            in_specs=[in_vmem] * 3,
            out_specs=in_vmem,
            out_shape=summed,
            compiler_params=params,
            cost_estimate=pl.CostEstimate(flops=(1 - part) * 2_000_000_000 + 1, bytes_accessed=100_000, transcendentals=0),
            name="expand",
        )(own, other, last)

    def swap(x, axis, size, mask):
        return lax.ppermute(x, axis, [(i, i ^ mask) for i in range(size)])

    def exchange(parts, *after):
        return [parts[0]] + [swap(tie(parts[k], *after) if after else parts[k], "seg", n_seg, k) for k in range(1, n_seg)]

    def total(terms, low, high):
        return functools.reduce(jnp.add, [x[low:high] for x in terms])

    def next_send(terms):
        left = terms[-1].shape[0]
        return total(terms, left // 2, left)

    parts = column_side(0, 1, mid, 53)
    received = {0: exchange(parts[0])}
    parts += column_side(1, chunks - 1, tie(mid, parts[0][-1]), 52)
    received[1] = exchange(parts[1])
    wide, expand_copy = row_weights()
    last_wide = expand_weights(swap(expand_copy, "tile", n_tile, 1))

    terms, sends, lows = [], {}, []
    last = chunks - 1

    def forward(group, b, *after):
        for c in group:
            terms[c][-1] = tie(terms[c][-1], *after)
        send = jnp.concatenate([next_send(terms[c]) for c in group])
        sends[group[-1], b] = send
        got = swap(send, "tile", n_tile, 1 << b)
        rows = got.shape[0] // len(group)
        for k, c in enumerate(group):
            terms[c].append(got[k * rows:(k + 1) * rows])
        return send

    def low_half(c, *after):
        own, other = lows[c]
        terms[c][0] = expanded(0, own, tie(other, *after), last_wide)
        return terms[c][0]

    for c in range(chunks):
        after = [sends[c - 1, 1]] if c else [parts[-1][0]]
        own_low, own_high, low, high = row_side([tie(x, *after) for x in received[c]], wide)
        lows.append((own_low, swap(low, "tile", n_tile, 1)))
        done = []
        if c >= 1:
            done.append(low_half(c - 1, own_high))
        if c >= 2:
            done.append(forward([c - 2], 2, own_high))
        got = swap(high, "tile", n_tile, 1)
        if done:
            got = tie(got, *done)
        sends[c, 1] = expanded(1, own_high, got, last_wide)
        terms.append([None, swap(sends[c, 1], "tile", n_tile, 2)])
        if c + 2 < chunks:
            received[c + 2] = exchange(parts[c + 2], own_high)
    low_half(last, sends[last, 1])
    done = [sends[last, 1]]
    for c, b in ((last - 3, 3), (last - 1, 2), (last - 2, 3), (last, 2), (last - 1, 3), (last, 3)):
        if b < bits and (c, b) not in sends:
            done = [forward([c], b, *done)]
    done = done[0]
    for b in range(4, bits):
        for c in range(chunks):
            done = forward([c], b, done)
    for c in range(last):
        terms[c][-1] = tie(terms[c][-1], sends[last, bits - 1])
    return jnp.concatenate([total(t, 0, out_rows) for t in terms], axis=1)


def solution(mesh):
    in_specs = (
        P(("tile", "seg"), None),
        P("tile", "seg", None, None),
        P("tile", None, "seg", None, None),
        P("tile", "seg", None, None),
        P("tile", None, "seg", None, None),
        P("tile", "seg", None, None),
    )
    out_specs = P(("seg", "tile"), None)
    body = functools.partial(shards, mesh.shape["tile"], mesh.shape["seg"])
    return jax.shard_map(body, mesh=mesh, in_specs=in_specs, out_specs=out_specs, check_vma=False)
```

profile of v0, /device:TPU:0, one launch (start us, length us, event | category | flops | bytes accessed | tf_op | source)
XLA Modules:
  0.0 57.2 jit_solution(12836120513735050455)
XLA Ops:
  0.0 3.7 %column_side.2 = (f32[512,128]{1,0:T(8,128)S(1)}, f32[512,128]{1,0:T(8,128)S(1)}) custom-call(f32[2048,512]{1,0:T(8,128)} %x_hbm.3, f32[16,64,128]{2,1,0:T(8,128)} %bitcast.12, f32[4,8,128,128]{3,2,1,0:T(8,128)} %bitcast.10, f32[16,64,64]{2,1,0:T(8,128)} %bitcast.14), custom_call_target="tpu_custom_call" | custom-call | flops 1000000 | bytes 100000 | tf_op jit(solution)/shard_map/column_side/pallas_call | solution.py:217
  3.7 0.0 copy-start
  3.7 0.0 copy-start.1
  3.7 3.0 %collective-permute-start = (f32[512,128]{1,0:T(8,128)S(1)}, f32[512,128]{1,0:T(8,128)S(1)}, u32[]{:S(2)}, u32[]{:S(2)}) collective-permute-start(f32[512,128]{1,0:T(8,128)S(1)} %get-tuple-element.61), channel_id=1, source_target_pairs={{0,1},{1,0},{2,3},{3,2},{4,5},{5,4},{6,7},{7,6},{8,9},{9,8},{10,11... | collective-permute-start | bytes 786440 | tf_op jit(solution)/shard_map/ppermute | solution.py:286
  6.7 5.8 %column_side.3 = (f32[512,128]{1,0:T(8,128)S(1)}, f32[512,128]{1,0:T(8,128)S(1)}, f32[512,128]{1,0:T(8,128)S(1)}, f32[512,128]{1,0:T(8,128)S(1)}, f32[512,128]{1,0:T(8,128)S(1)}, /*index=5*/f32[512,128]{1,0:T(8,128)S(1)}) custom-call(f32[2048,512]{1,0:T(8,128)} %x_hbm.3, f32[16,64,128]{2,1,0:T(8,128)} %bitcast.13, f32[4,8,128,128]{3,2,1,0:T(8,128)} %bitcast.11, ...), custom_call_target="tpu_custom_call" | custom-call | flops 1000000 | bytes 100000 | tf_op jit(solution)/shard_map/column_side/pallas_call | solution.py:217
  12.5 0.2 collective-permute-start.4
  12.8 0.3 row_weights.1
  13.1 0.1 collective-permute-start.3
  13.1 0.0 collective-permute-done.refs_1_
  13.2 1.2 %row_side.4 = (f32[256,128]{1,0:T(8,128)S(1)}, f32[256,128]{1,0:T(8,128)S(1)}, f32[256,128]{1,0:T(8,128)S(1)}, f32[256,128]{1,0:T(8,128)S(1)}) custom-call(f32[512,128]{1,0:T(8,128)S(1)} %get-tuple-element.64.refs_0_, f32[512,128]{1,0:T(8,128)S(1)} %collective-permute-done.refs_1_, bf16[4,8,128,256]{3,2,1,0:T(8,128)(2,1)S(1)} %get-tuple-element.66.refs_2_), custom_call_target="tpu_custom_call" | custom-call | flops 20000000000 | bytes 100000 | tf_op jit(solution)/shard_map/row_side/pallas_call | solution.py:263
  14.3 0.6 collective-permute-start.2
  14.9 0.1 collective-permute-start.1
  15.0 1.9 %collective-permute-start.7 = (f32[512,128]{1,0:T(8,128)S(1)}, f32[512,128]{1,0:T(8,128)S(1)}, u32[]{:S(2)}, u32[]{:S(2)}) collective-permute-start(f32[512,128]{1,0:T(8,128)S(1)} %get-tuple-element.83), channel_id=1, source_target_pairs={{0,1},{1,0},{2,3},{3,2},{4,5},{5,4},{6,7},{7,6},{8,9},{9,8},{10,11... | collective-permute-start | bytes 786440 | tf_op jit(solution)/shard_map/ppermute | solution.py:286
  16.8 0.0 collective-permute-done.3.other_ref
  16.9 0.2 expand_weights.1.last_ref
  17.1 0.0 collective-permute-done.2.other_ref
  17.1 0.2 expand.8
  17.3 1.6 %collective-permute-start.5 = (f32[512,128]{1,0:T(8,128)S(1)}, f32[512,128]{1,0:T(8,128)S(1)}, u32[]{:S(2)}, u32[]{:S(2)}) collective-permute-start(f32[512,128]{1,0:T(8,128)S(1)} %expand.8), channel_id=1, source_target_pairs={{0,4},{2,6},{4,0},{6,2},{8,12},{10,14},{12,8},{14,10},{16,20},{18,... | collective-permute-start | bytes 786440 | tf_op jit(solution)/shard_map/ppermute | solution.py:286
  18.9 2.9 %collective-permute-done.4.refs_1_ = f32[512,128]{1,0:T(8,128)S(1)} collective-permute-done((f32[512,128]{1,0:T(8,128)S(1)}, f32[512,128]{1,0:T(8,128)S(1)}, u32[]{:S(2)}, u32[]{:S(2)}) %collective-permute-start.4) | collective-permute-done | bytes 262176 | tf_op jit(solution)/shard_map/ppermute | solution.py:286
  21.8 1.2 %row_side.5 = (f32[256,128]{1,0:T(8,128)S(1)}, f32[256,128]{1,0:T(8,128)S(1)}, f32[256,128]{1,0:T(8,128)S(1)}, f32[256,128]{1,0:T(8,128)S(1)}) custom-call(f32[512,128]{1,0:T(8,128)S(1)} %get-tuple-element.73.refs_0_, f32[512,128]{1,0:T(8,128)S(1)} %collective-permute-done.4.refs_1_, bf16[4,8,128,256]{3,2,1,0:T(8,128)(2,1)S(1)} %get-tuple-element.66.refs_2_), custom_call_target="tpu_custom_call" | custom-call | flops 20000000000 | bytes 100000 | tf_op jit(solution)/shard_map/row_side/pallas_call | solution.py:263
  23.0 0.0 collective-permute-done.1.other_ref
  23.0 0.1 collective-permute-start.6
  23.1 0.5 collective-permute-start.10
  23.6 0.0 collective-permute-start.11
  23.6 0.2 expand.9
  23.9 0.6 %collective-permute-done.6.other_ref = f32[256,128]{1,0:T(8,128)S(1)} collective-permute-done((f32[256,128]{1,0:T(8,128)S(1)}, f32[256,128]{1,0:T(8,128)S(1)}, u32[]{:S(2)}, u32[]{:S(2)}) %collective-permute-start.6) | collective-permute-done | bytes 131104 | tf_op jit(solution)/shard_map/ppermute | solution.py:286
  24.5 0.2 expand.10
  24.7 1.6 %collective-permute-start.14 = (f32[512,128]{1,0:T(8,128)S(1)}, f32[512,128]{1,0:T(8,128)S(1)}, u32[]{:S(2)}, u32[]{:S(2)}) collective-permute-start(f32[512,128]{1,0:T(8,128)S(1)} %expand.10), channel_id=1, source_target_pairs={{0,4},{2,6},{4,0},{6,2},{8,12},{10,14},{12,8},{14,10},{16,20},{18,... | collective-permute-start | bytes 786440 | tf_op jit(solution)/shard_map/ppermute | solution.py:286
  26.3 0.0 collective-permute-done.7.refs_1_
  26.3 1.2 %row_side.6 = (f32[256,128]{1,0:T(8,128)S(1)}, f32[256,128]{1,0:T(8,128)S(1)}, f32[256,128]{1,0:T(8,128)S(1)}, f32[256,128]{1,0:T(8,128)S(1)}) custom-call(f32[512,128]{1,0:T(8,128)S(1)} %get-tuple-element.81.refs_0_, f32[512,128]{1,0:T(8,128)S(1)} %collective-permute-done.7.refs_1_, bf16[4,8,128,256]{3,2,1,0:T(8,128)(2,1)S(1)} %get-tuple-element.66.refs_2_), custom_call_target="tpu_custom_call" | custom-call | flops 20000000000 | bytes 100000 | tf_op jit(solution)/shard_map/row_side/pallas_call | solution.py:263
  27.5 0.1 collective-permute-start.9
  27.6 0.0 collective-permute-done.10.other_ref
  27.6 0.5 collective-permute-start.13
  28.1 0.2 expand.11
  28.3 1.6 %collective-permute-start.8 = (f32[256,128]{1,0:T(8,128)S(1)}, f32[256,128]{1,0:T(8,128)S(1)}, u32[]{:S(2)}, u32[]{:S(2)}) collective-permute-start(f32[256,128]{1,0:T(8,128)S(1)} %slice_add_fusion.3), channel_id=1, source_target_pairs={{0,8},{2,10},{4,12},{6,14},{8,0},{10,2},{12,4},{14,6},{16,24},{18,... | collective-permute-start | bytes 393224 | tf_op jit(solution)/shard_map/ppermute | solution.py:286
  30.0 0.0 collective-permute-done.9.other_ref
  30.0 0.2 expand.12
  30.2 1.3 %collective-permute-start.19 = (f32[512,128]{1,0:T(8,128)S(1)}, f32[512,128]{1,0:T(8,128)S(1)}, u32[]{:S(2)}, u32[]{:S(2)}) collective-permute-start(f32[512,128]{1,0:T(8,128)S(1)} %expand.12), channel_id=1, source_target_pairs={{0,4},{2,6},{4,0},{6,2},{8,12},{10,14},{12,8},{14,10},{16,20},{18,... | collective-permute-start | bytes 786440 | tf_op jit(solution)/shard_map/ppermute | solution.py:286
  31.5 0.4 collective-permute-done.11.refs_1_
  31.9 1.2 %row_side.7 = (f32[256,128]{1,0:T(8,128)S(1)}, f32[256,128]{1,0:T(8,128)S(1)}, f32[256,128]{1,0:T(8,128)S(1)}, f32[256,128]{1,0:T(8,128)S(1)}) custom-call(f32[512,128]{1,0:T(8,128)S(1)} %get-tuple-element.92.refs_0_, f32[512,128]{1,0:T(8,128)S(1)} %collective-permute-done.11.refs_1_, bf16[4,8,128,256]{3,2,1,0:T(8,128)(2,1)S(1)} %get-tuple-element.66.refs_2_), custom_call_target="tpu_custom_call" | custom-call | flops 20000000000 | bytes 100000 | tf_op jit(solution)/shard_map/row_side/pallas_call | solution.py:263
  33.1 0.0 collective-permute-done.13.other_ref
  33.1 0.1 collective-permute-start.12
  33.2 0.5 collective-permute-start.16
  33.7 0.2 expand.13
  34.0 1.6 %collective-permute-start.18 = (f32[256,128]{1,0:T(8,128)S(1)}, f32[256,128]{1,0:T(8,128)S(1)}, u32[]{:S(2)}, u32[]{:S(2)}) collective-permute-start(f32[256,128]{1,0:T(8,128)S(1)} %slice_add_fusion.2), channel_id=1, source_target_pairs={{0,8},{2,10},{4,12},{6,14},{8,0},{10,2},{12,4},{14,6},{16,24},{18,... | collective-permute-start | bytes 393224 | tf_op jit(solution)/shard_map/ppermute | solution.py:286
  35.6 0.2 expand.14
  35.8 1.6 %collective-permute-start.17 = (f32[512,128]{1,0:T(8,128)S(1)}, f32[512,128]{1,0:T(8,128)S(1)}, u32[]{:S(2)}, u32[]{:S(2)}) collective-permute-start(f32[512,128]{1,0:T(8,128)S(1)} %expand.14), channel_id=1, source_target_pairs={{0,4},{2,6},{4,0},{6,2},{8,12},{10,14},{12,8},{14,10},{16,20},{18,... | collective-permute-start | bytes 786440 | tf_op jit(solution)/shard_map/ppermute | solution.py:286
  37.4 0.0 collective-permute-done.8
  37.5 0.0 collective-permute-done.16.other_ref
  37.5 2.7 %collective-permute-start.15 = (f32[128,128]{1,0:T(8,128)S(1)}, f32[128,128]{1,0:T(8,128)S(1)}, u32[]{:S(2)}, u32[]{:S(2)}) collective-permute-start(f32[128,128]{1,0:T(8,128)S(1)} %fusion.9), channel_id=1, source_target_pairs={{0,16},{2,18},{4,20},{6,22},{8,24},{10,26},{12,28},{14,30},{16,0},... | collective-permute-start | bytes 196616 | tf_op jit(solution)/shard_map/ppermute | solution.py:286
  40.1 0.2 expand.15
  40.4 0.8 %collective-permute-start.21 = (f32[256,128]{1,0:T(8,128)S(1)}, f32[256,128]{1,0:T(8,128)S(1)}, u32[]{:S(2)}, u32[]{:S(2)}) collective-permute-start(f32[256,128]{1,0:T(8,128)S(1)} %slice_add_fusion.1), channel_id=1, source_target_pairs={{0,8},{2,10},{4,12},{6,14},{8,0},{10,2},{12,4},{14,6},{16,24},{18,... | collective-permute-start | bytes 393224 | tf_op jit(solution)/shard_map/ppermute | solution.py:286
  41.2 0.0 collective-permute-done.18
  41.2 2.7 %collective-permute-start.22 = (f32[128,128]{1,0:T(8,128)S(1)}, f32[128,128]{1,0:T(8,128)S(1)}, u32[]{:S(2)}, u32[]{:S(2)}) collective-permute-start(f32[128,128]{1,0:T(8,128)S(1)} %fusion.7), channel_id=1, source_target_pairs={{0,16},{2,18},{4,20},{6,22},{8,24},{10,26},{12,28},{14,30},{16,0},... | collective-permute-start | bytes 196616 | tf_op jit(solution)/shard_map/ppermute | solution.py:286
  43.9 0.5 collective-permute-done.17
  44.4 1.6 %collective-permute-start.20 = (f32[256,128]{1,0:T(8,128)S(1)}, f32[256,128]{1,0:T(8,128)S(1)}, u32[]{:S(2)}, u32[]{:S(2)}) collective-permute-start(f32[256,128]{1,0:T(8,128)S(1)} %slice_add_fusion), channel_id=1, source_target_pairs={{0,8},{2,10},{4,12},{6,14},{8,0},{10,2},{12,4},{14,6},{16,24},{18,... | collective-permute-start | bytes 393224 | tf_op jit(solution)/shard_map/ppermute | solution.py:286
  46.0 1.4 %collective-permute-done.21 = f32[256,128]{1,0:T(8,128)S(1)} collective-permute-done((f32[256,128]{1,0:T(8,128)S(1)}, f32[256,128]{1,0:T(8,128)S(1)}, u32[]{:S(2)}, u32[]{:S(2)}) %collective-permute-start.21) | collective-permute-done | bytes 131104 | tf_op jit(solution)/shard_map/ppermute | solution.py:286
  47.5 1.2 %collective-permute-start.23 = (f32[128,128]{1,0:T(8,128)S(1)}, f32[128,128]{1,0:T(8,128)S(1)}, u32[]{:S(2)}, u32[]{:S(2)}) collective-permute-start(f32[128,128]{1,0:T(8,128)S(1)} %fusion.6), channel_id=1, source_target_pairs={{0,16},{2,18},{4,20},{6,22},{8,24},{10,26},{12,28},{14,30},{16,0},... | collective-permute-start | bytes 196616 | tf_op jit(solution)/shard_map/ppermute | solution.py:286
  48.7 1.8 %collective-permute-done.20 = f32[256,128]{1,0:T(8,128)S(1)} collective-permute-done((f32[256,128]{1,0:T(8,128)S(1)}, f32[256,128]{1,0:T(8,128)S(1)}, u32[]{:S(2)}, u32[]{:S(2)}) %collective-permute-start.20) | collective-permute-done | bytes 131104 | tf_op jit(solution)/shard_map/ppermute | solution.py:286
  50.6 2.0 %collective-permute-start.24 = (f32[128,128]{1,0:T(8,128)S(1)}, f32[128,128]{1,0:T(8,128)S(1)}, u32[]{:S(2)}, u32[]{:S(2)}) collective-permute-start(f32[128,128]{1,0:T(8,128)S(1)} %fusion.8), channel_id=1, source_target_pairs={{0,16},{2,18},{4,20},{6,22},{8,24},{10,26},{12,28},{14,30},{16,0},... | collective-permute-start | bytes 196616 | tf_op jit(solution)/shard_map/ppermute | solution.py:286
  52.6 0.0 collective-permute-done.22
  52.6 2.1 %collective-permute-done.23 = f32[128,128]{1,0:T(8,128)S(1)} collective-permute-done((f32[128,128]{1,0:T(8,128)S(1)}, f32[128,128]{1,0:T(8,128)S(1)}, u32[]{:S(2)}, u32[]{:S(2)}) %collective-permute-start.23) | collective-permute-done | bytes 65568 | tf_op jit(solution)/shard_map/ppermute | solution.py:286
  54.7 1.8 %collective-permute-done.24 = f32[128,128]{1,0:T(8,128)S(1)} collective-permute-done((f32[128,128]{1,0:T(8,128)S(1)}, f32[128,128]{1,0:T(8,128)S(1)}, u32[]{:S(2)}, u32[]{:S(2)}) %collective-permute-start.24) | collective-permute-done | bytes 65568 | tf_op jit(solution)/shard_map/ppermute | solution.py:286
  56.5 0.7 %pad_maximum_fusion = f32[128,512]{1,0:T(8,128)} fusion(f32[128,128]{1,0:T(8,128)S(1)} %fusion.1, f32[128,128]{1,0:T(8,128)S(1)} %fusion.3, f32[128,128]{1,0:T(8,128)S(1)} %fusion.5, f32[128,128]{1,0:T(8,128)S(1)} %fusion.11), kind=kLoop, calls=%fused_computation | loop fusion | flops 196608 | bytes 524288 | tf_op jit(solution)/shard_map/concatenate | solution.py:351
  (19 shorter events, 0.2 us)
Async XLA Ops:
  3.7 9.1 %copy-start = (f32[1,16,128,64]{2,3,1,0:T(8,128)S(1)}, f32[1,16,128,64]{2,3,1,0:T(8,128)}, u32[]{:S(2)}) copy-start(f32[1,16,128,64]{2,3,1,0:T(8,128)} %param.11) | copy-start | bytes 1572868
  3.7 9.1 %copy-start.1 = (f32[1,4,8,128,128]{4,3,2,1,0:T(8,128)S(1)}, f32[1,4,8,128,128]{4,3,2,1,0:T(8,128)}, u32[]{:S(2)}) copy-start(f32[1,4,8,128,128]{4,3,2,1,0:T(8,128)} %param.10) | copy-start | bytes 6291460
  3.7 9.4 %collective-permute-start = (f32[512,128]{1,0:T(8,128)S(1)}, f32[512,128]{1,0:T(8,128)S(1)}, u32[]{:S(2)}, u32[]{:S(2)}) collective-permute-start(f32[512,128]{1,0:T(8,128)S(1)} %get-tuple-element.61), channel_id=1, source_target_pairs={{0,1},{1,0},{2,3},{3,2},{4,5},{5,4},{6,7},{7,6},{8,9},{9,8},{10,11... | collective-permute-start | bytes 786440 | tf_op jit(solution)/shard_map/ppermute | solution.py:286
  12.5 9.3 %collective-permute-start.4 = (f32[512,128]{1,0:T(8,128)S(1)}, f32[512,128]{1,0:T(8,128)S(1)}, u32[]{:S(2)}, u32[]{:S(2)}) collective-permute-start(f32[512,128]{1,0:T(8,128)S(1)} %get-tuple-element.74), channel_id=1, source_target_pairs={{0,1},{1,0},{2,3},{3,2},{4,5},{5,4},{6,7},{7,6},{8,9},{9,8},{10,11... | collective-permute-start | bytes 786440 | tf_op jit(solution)/shard_map/ppermute | solution.py:286
  13.1 3.8 %collective-permute-start.3 = (f32[16,64,128]{2,1,0:T(8,128)S(1)}, f32[16,64,128]{2,1,0:T(8,128)S(1)}, u32[]{:S(2)}, u32[]{:S(2)}) collective-permute-start(f32[16,64,128]{2,1,0:T(8,128)S(1)} %get-tuple-element.72), channel_id=1, source_target_pairs={{0,2},{2,0},{4,6},{6,4},{8,10},{10,8},{12,14},{14,12},{16,18},{18,... | collective-permute-start | bytes 1572872 | tf_op jit(solution)/shard_map/ppermute | solution.py:286
  14.3 2.7 %collective-permute-start.2 = (f32[256,128]{1,0:T(8,128)S(1)}, f32[256,128]{1,0:T(8,128)S(1)}, u32[]{:S(2)}, u32[]{:S(2)}) collective-permute-start(f32[256,128]{1,0:T(8,128)S(1)} %get-tuple-element.71), channel_id=1, source_target_pairs={{0,2},{2,0},{4,6},{6,4},{8,10},{10,8},{12,14},{14,12},{16,18},{18,... | collective-permute-start | bytes 393224 | tf_op jit(solution)/shard_map/ppermute | solution.py:286
  14.9 8.1 %collective-permute-start.1 = (f32[256,128]{1,0:T(8,128)S(1)}, f32[256,128]{1,0:T(8,128)S(1)}, u32[]{:S(2)}, u32[]{:S(2)}) collective-permute-start(f32[256,128]{1,0:T(8,128)S(1)} %get-tuple-element.68), channel_id=1, source_target_pairs={{0,2},{2,0},{4,6},{6,4},{8,10},{10,8},{12,14},{14,12},{16,18},{18,... | collective-permute-start | bytes 393224 | tf_op jit(solution)/shard_map/ppermute | solution.py:286
  15.0 11.3 %collective-permute-start.7 = (f32[512,128]{1,0:T(8,128)S(1)}, f32[512,128]{1,0:T(8,128)S(1)}, u32[]{:S(2)}, u32[]{:S(2)}) collective-permute-start(f32[512,128]{1,0:T(8,128)S(1)} %get-tuple-element.83), channel_id=1, source_target_pairs={{0,1},{1,0},{2,3},{3,2},{4,5},{5,4},{6,7},{7,6},{8,9},{9,8},{10,11... | collective-permute-start | bytes 786440 | tf_op jit(solution)/shard_map/ppermute | solution.py:286
  17.3 11.0 %collective-permute-start.5 = (f32[512,128]{1,0:T(8,128)S(1)}, f32[512,128]{1,0:T(8,128)S(1)}, u32[]{:S(2)}, u32[]{:S(2)}) collective-permute-start(f32[512,128]{1,0:T(8,128)S(1)} %expand.8), channel_id=1, source_target_pairs={{0,4},{2,6},{4,0},{6,2},{8,12},{10,14},{12,8},{14,10},{16,20},{18,... | collective-permute-start | bytes 786440 | tf_op jit(solution)/shard_map/ppermute | solution.py:286
  23.0 1.4 %collective-permute-start.6 = (f32[256,128]{1,0:T(8,128)S(1)}, f32[256,128]{1,0:T(8,128)S(1)}, u32[]{:S(2)}, u32[]{:S(2)}) collective-permute-start(f32[256,128]{1,0:T(8,128)S(1)} %get-tuple-element.79), channel_id=1, source_target_pairs={{0,2},{2,0},{4,6},{6,4},{8,10},{10,8},{12,14},{14,12},{16,18},{18,... | collective-permute-start | bytes 393224 | tf_op jit(solution)/shard_map/ppermute | solution.py:286
  23.1 4.4 %collective-permute-start.10 = (f32[256,128]{1,0:T(8,128)S(1)}, f32[256,128]{1,0:T(8,128)S(1)}, u32[]{:S(2)}, u32[]{:S(2)}) collective-permute-start(f32[256,128]{1,0:T(8,128)S(1)} %get-tuple-element.89), channel_id=1, source_target_pairs={{0,2},{2,0},{4,6},{6,4},{8,10},{10,8},{12,14},{14,12},{16,18},{18,... | collective-permute-start | bytes 393224 | tf_op jit(solution)/shard_map/ppermute | solution.py:286
  23.6 8.3 %collective-permute-start.11 = (f32[512,128]{1,0:T(8,128)S(1)}, f32[512,128]{1,0:T(8,128)S(1)}, u32[]{:S(2)}, u32[]{:S(2)}) collective-permute-start(f32[512,128]{1,0:T(8,128)S(1)} %get-tuple-element.94), channel_id=1, source_target_pairs={{0,1},{1,0},{2,3},{3,2},{4,5},{5,4},{6,7},{7,6},{8,9},{9,8},{10,11... | collective-permute-start | bytes 786440 | tf_op jit(solution)/shard_map/ppermute | solution.py:286
  24.7 9.2 %collective-permute-start.14 = (f32[512,128]{1,0:T(8,128)S(1)}, f32[512,128]{1,0:T(8,128)S(1)}, u32[]{:S(2)}, u32[]{:S(2)}) collective-permute-start(f32[512,128]{1,0:T(8,128)S(1)} %expand.10), channel_id=1, source_target_pairs={{0,4},{2,6},{4,0},{6,2},{8,12},{10,14},{12,8},{14,10},{16,20},{18,... | collective-permute-start | bytes 786440 | tf_op jit(solution)/shard_map/ppermute | solution.py:286
  27.5 2.5 %collective-permute-start.9 = (f32[256,128]{1,0:T(8,128)S(1)}, f32[256,128]{1,0:T(8,128)S(1)}, u32[]{:S(2)}, u32[]{:S(2)}) collective-permute-start(f32[256,128]{1,0:T(8,128)S(1)} %get-tuple-element.87), channel_id=1, source_target_pairs={{0,2},{2,0},{4,6},{6,4},{8,10},{10,8},{12,14},{14,12},{16,18},{18,... | collective-permute-start | bytes 393224 | tf_op jit(solution)/shard_map/ppermute | solution.py:286
  27.6 5.5 %collective-permute-start.13 = (f32[256,128]{1,0:T(8,128)S(1)}, f32[256,128]{1,0:T(8,128)S(1)}, u32[]{:S(2)}, u32[]{:S(2)}) collective-permute-start(f32[256,128]{1,0:T(8,128)S(1)} %get-tuple-element.99), channel_id=1, source_target_pairs={{0,2},{2,0},{4,6},{6,4},{8,10},{10,8},{12,14},{14,12},{16,18},{18,... | collective-permute-start | bytes 393224 | tf_op jit(solution)/shard_map/ppermute | solution.py:286
  28.3 9.1 %collective-permute-start.8 = (f32[256,128]{1,0:T(8,128)S(1)}, f32[256,128]{1,0:T(8,128)S(1)}, u32[]{:S(2)}, u32[]{:S(2)}) collective-permute-start(f32[256,128]{1,0:T(8,128)S(1)} %slice_add_fusion.3), channel_id=1, source_target_pairs={{0,8},{2,10},{4,12},{6,14},{8,0},{10,2},{12,4},{14,6},{16,24},{18,... | collective-permute-start | bytes 393224 | tf_op jit(solution)/shard_map/ppermute | solution.py:286
  30.2 10.1 %collective-permute-start.19 = (f32[512,128]{1,0:T(8,128)S(1)}, f32[512,128]{1,0:T(8,128)S(1)}, u32[]{:S(2)}, u32[]{:S(2)}) collective-permute-start(f32[512,128]{1,0:T(8,128)S(1)} %expand.12), channel_id=1, source_target_pairs={{0,4},{2,6},{4,0},{6,2},{8,12},{10,14},{12,8},{14,10},{16,20},{18,... | collective-permute-start | bytes 786440 | tf_op jit(solution)/shard_map/ppermute | solution.py:286
  33.1 2.5 %collective-permute-start.12 = (f32[256,128]{1,0:T(8,128)S(1)}, f32[256,128]{1,0:T(8,128)S(1)}, u32[]{:S(2)}, u32[]{:S(2)}) collective-permute-start(f32[256,128]{1,0:T(8,128)S(1)} %get-tuple-element.97), channel_id=1, source_target_pairs={{0,2},{2,0},{4,6},{6,4},{8,10},{10,8},{12,14},{14,12},{16,18},{18,... | collective-permute-start | bytes 393224 | tf_op jit(solution)/shard_map/ppermute | solution.py:286
  33.2 4.3 %collective-permute-start.16 = (f32[256,128]{1,0:T(8,128)S(1)}, f32[256,128]{1,0:T(8,128)S(1)}, u32[]{:S(2)}, u32[]{:S(2)}) collective-permute-start(f32[256,128]{1,0:T(8,128)S(1)} %get-tuple-element.105), channel_id=1, source_target_pairs={{0,2},{2,0},{4,6},{6,4},{8,10},{10,8},{12,14},{14,12},{16,18},{18,... | collective-permute-start | bytes 393224 | tf_op jit(solution)/shard_map/ppermute | solution.py:286
  34.0 7.2 %collective-permute-start.18 = (f32[256,128]{1,0:T(8,128)S(1)}, f32[256,128]{1,0:T(8,128)S(1)}, u32[]{:S(2)}, u32[]{:S(2)}) collective-permute-start(f32[256,128]{1,0:T(8,128)S(1)} %slice_add_fusion.2), channel_id=1, source_target_pairs={{0,8},{2,10},{4,12},{6,14},{8,0},{10,2},{12,4},{14,6},{16,24},{18,... | collective-permute-start | bytes 393224 | tf_op jit(solution)/shard_map/ppermute | solution.py:286
  35.8 8.5 %collective-permute-start.17 = (f32[512,128]{1,0:T(8,128)S(1)}, f32[512,128]{1,0:T(8,128)S(1)}, u32[]{:S(2)}, u32[]{:S(2)}) collective-permute-start(f32[512,128]{1,0:T(8,128)S(1)} %expand.14), channel_id=1, source_target_pairs={{0,4},{2,6},{4,0},{6,2},{8,12},{10,14},{12,8},{14,10},{16,20},{18,... | collective-permute-start | bytes 786440 | tf_op jit(solution)/shard_map/ppermute | solution.py:286
  37.5 15.1 %collective-permute-start.15 = (f32[128,128]{1,0:T(8,128)S(1)}, f32[128,128]{1,0:T(8,128)S(1)}, u32[]{:S(2)}, u32[]{:S(2)}) collective-permute-start(f32[128,128]{1,0:T(8,128)S(1)} %fusion.9), channel_id=1, source_target_pairs={{0,16},{2,18},{4,20},{6,22},{8,24},{10,26},{12,28},{14,30},{16,0},... | collective-permute-start | bytes 196616 | tf_op jit(solution)/shard_map/ppermute | solution.py:286
  40.4 7.0 %collective-permute-start.21 = (f32[256,128]{1,0:T(8,128)S(1)}, f32[256,128]{1,0:T(8,128)S(1)}, u32[]{:S(2)}, u32[]{:S(2)}) collective-permute-start(f32[256,128]{1,0:T(8,128)S(1)} %slice_add_fusion.1), channel_id=1, source_target_pairs={{0,8},{2,10},{4,12},{6,14},{8,0},{10,2},{12,4},{14,6},{16,24},{18,... | collective-permute-start | bytes 393224 | tf_op jit(solution)/shard_map/ppermute | solution.py:286
  41.2 11.4 %collective-permute-start.22 = (f32[128,128]{1,0:T(8,128)S(1)}, f32[128,128]{1,0:T(8,128)S(1)}, u32[]{:S(2)}, u32[]{:S(2)}) collective-permute-start(f32[128,128]{1,0:T(8,128)S(1)} %fusion.7), channel_id=1, source_target_pairs={{0,16},{2,18},{4,20},{6,22},{8,24},{10,26},{12,28},{14,30},{16,0},... | collective-permute-start | bytes 196616 | tf_op jit(solution)/shard_map/ppermute | solution.py:286
  44.4 6.2 %collective-permute-start.20 = (f32[256,128]{1,0:T(8,128)S(1)}, f32[256,128]{1,0:T(8,128)S(1)}, u32[]{:S(2)}, u32[]{:S(2)}) collective-permute-start(f32[256,128]{1,0:T(8,128)S(1)} %slice_add_fusion), channel_id=1, source_target_pairs={{0,8},{2,10},{4,12},{6,14},{8,0},{10,2},{12,4},{14,6},{16,24},{18,... | collective-permute-start | bytes 393224 | tf_op jit(solution)/shard_map/ppermute | solution.py:286
  47.5 7.2 %collective-permute-start.23 = (f32[128,128]{1,0:T(8,128)S(1)}, f32[128,128]{1,0:T(8,128)S(1)}, u32[]{:S(2)}, u32[]{:S(2)}) collective-permute-start(f32[128,128]{1,0:T(8,128)S(1)} %fusion.6), channel_id=1, source_target_pairs={{0,16},{2,18},{4,20},{6,22},{8,24},{10,26},{12,28},{14,30},{16,0},... | collective-permute-start | bytes 196616 | tf_op jit(solution)/shard_map/ppermute | solution.py:286
  50.6 5.9 %collective-permute-start.24 = (f32[128,128]{1,0:T(8,128)S(1)}, f32[128,128]{1,0:T(8,128)S(1)}, u32[]{:S(2)}, u32[]{:S(2)}) collective-permute-start(f32[128,128]{1,0:T(8,128)S(1)} %fusion.8), channel_id=1, source_target_pairs={{0,16},{2,18},{4,20},{6,22},{8,24},{10,26},{12,28},{14,30},{16,0},... | collective-permute-start | bytes 196616 | tf_op jit(solution)/shard_map/ppermute | solution.py:286
where the time goes:
time: 57.4 us; the launch traced here: 57.2 us
  starting transfers between devices  27.8 us (48%)
  Pallas kernels  16.6 us (29%)
  waiting for transfers between devices  11.6 us (20%)
  other arithmetic  0.9 us (2%)
    ppermute x25, starting transfers between devices, swap(): return lax.ppermute(x, axis, [(i, i ^ mask) for i in range(size)])  27.8 us
    ppermute x25, waiting for transfers between devices, swap(): return lax.ppermute(x, axis, [(i, i ^ mask) for i in range(size)])  11.6 us
    pallas_call x2, Pallas kernels, column_side(): pl.pallas_call(functools.partial(column_kernel, n_seg, pieces, start * CH...  9.5 us
    pallas_call x4, Pallas kernels, row_side(): pl.pallas_call(functools.partial(row_kernel, n_seg, n_tile, leaf), in_spe...  4.71 us
    pallas_call x8, Pallas kernels, expanded(): pl.pallas_call(functools.partial(expand_kernel, part), in_specs=[in_vmem]...  1.89 us
  transfers between devices with their start and end apart: 25, of which 8 were waited for; matrix products, arithmetic and copies ran while one was open for 0% of the time, Pallas kernels for 23%

commit v1 on v0

--- a/solution.py
+++ b/solution.py
@@ -23,17 +23,16 @@
 
 
 def wide_of(w):
-    return jnp.concatenate(split(w), axis=1)
+    return jnp.concatenate(split(w), axis=0)
 
 
 def product3(wide, v_hi, v_lo):
-    depth, width = v_hi.shape
+    rows, width = wide.shape[0] // 2, v_hi.shape[1]
     if width > CHUNK:
-        return dot(wide, jnp.concatenate([v_hi, v_hi], axis=0)) + dot(wide[:, :depth], v_lo)
-    left = jnp.concatenate([v_hi, v_hi], axis=0)
-    right = jnp.concatenate([v_lo, jnp.zeros_like(v_lo)], axis=0)
-    both = dot(wide, jnp.concatenate([left, right], axis=1))
-    return both[:, :width] + both[:, width:]
+        left = dot(wide, v_hi)
+        return left[:rows] + left[rows:] + dot(wide[:rows], v_lo)
+    both = dot(wide, jnp.concatenate([v_hi, v_lo], axis=1))
+    return both[:rows, :width] + both[rows:, :width] + both[:rows, width:]
 
 
 def pair_of(hi, lo, first, second, rank, cols=slice(None)):
@@ -59,7 +58,7 @@
 
 
 def project(n, wide, x, hi, lo, cuts):
-    rank, leaf = wide.shape[0], wide.shape[1] // 2
+    rank, leaf = wide.shape[0] // 2, wide.shape[1]
     for cols in cuts:
         c_hi, c_lo = split(product3(wide, *split(x[n * leaf:(n + 1) * leaf, cols])))
         hi[n * rank:(n + 1) * rank, cols] = c_hi
@@ -182,8 +181,8 @@
 
 
 def expand_kernel(part, own_ref, other_ref, last_ref, out_ref):
-    rank = last_ref.shape[2] // 4
-    unit = last_ref.shape[1]
+    rank = last_ref.shape[2] // 2
+    unit = last_ref.shape[1] // 2
     for k in range(own_ref.shape[0] // rank):
         rows = slice(k * rank, (k + 1) * rank)
         v = jnp.concatenate([own_ref[rows, :], other_ref[rows, :]], axis=0)
@@ -212,7 +211,7 @@
     in_vmem = pl.BlockSpec(memory_space=pltpu.VMEM)
 
     def column_side(start, count, mid, limit):
-        pieces = 4
+        pieces = 8
         width = count * CHUNK
         outs = pl.pallas_call(
             functools.partial(column_kernel, n_seg, pieces, start * CHUNK),
@@ -240,7 +239,7 @@
             in_specs=[in_vmem] * 2,
             out_specs=[in_vmem] * 2,
             out_shape=[
-                jax.ShapeDtypeStruct((levels, pairs, 2 * rank, 4 * rank), BF16),
+                jax.ShapeDtypeStruct((levels, pairs, 4 * rank, 2 * rank), BF16),
                 jax.ShapeDtypeStruct(expand.shape, F32),
             ],
             compiler_params=params,
@@ -253,7 +252,7 @@
             functools.partial(expand_weights_kernel, n_tile),
             in_specs=[in_vmem] * 2,
             out_specs=in_vmem,
-            out_shape=jax.ShapeDtypeStruct((n_tile // 2 * pieces, unit, 4 * rank), BF16),
+            out_shape=jax.ShapeDtypeStruct((n_tile // 2 * pieces, 2 * unit, 2 * rank), BF16),
             compiler_params=params,
             cost_estimate=cost,
             name="expand_weights",

time: 57.4 us -> 60.9 us (1.061)
  Pallas kernels: 16.6 us -> 21 us
  starting transfers between devices: 27.8 us -> 26 us
  waiting for transfers between devices: 11.6 us -> 12.5 us
    pallas_call x2, Pallas kernels: 9.5 us -> 12.3 us  [column_side(): pl.pallas_call(functools.partial(column_kernel, n_seg, pieces, start * CH...]
    ppermute x25, starting transfers between devices: 27.8 us -> 26 us  [swap(): return lax.ppermute(x, axis, [(i, i ^ mask) for i in range(size)])]
    pallas_call x4, Pallas kernels: 4.71 us -> 6 us  [row_side(): pl.pallas_call(functools.partial(row_kernel, n_seg, n_tile, leaf), in_spe...]
    ppermute x25, waiting for transfers between devices: 11.6 us -> 12.5 us  [swap(): return lax.ppermute(x, axis, [(i, i ^ mask) for i in range(size)])]
  transfers between devices with their start and end apart: 25 -> 25, of which waited for: 8 -> 8; matrix products, arithmetic and copies ran while one was open for 0% -> 0% of each run, Pallas kernels for 23% -> 27%
where the time goes in v1:
time: 60.9 us; the launch traced here: 60.7 us
  starting transfers between devices  26 us (43%)
  Pallas kernels  21 us (34%)
  waiting for transfers between devices  12.5 us (21%)
  other arithmetic  0.9 us (1%)
    ppermute x25, starting transfers between devices, swap(): return lax.ppermute(x, axis, [(i, i ^ mask) for i in range(size)])  26 us
    ppermute x25, waiting for transfers between devices, swap(): return lax.ppermute(x, axis, [(i, i ^ mask) for i in range(size)])  12.5 us
    pallas_call x2, Pallas kernels, column_side(): pl.pallas_call(functools.partial(column_kernel, n_seg, pieces, start * CH...  12.3 us
    pallas_call x4, Pallas kernels, row_side(): pl.pallas_call(functools.partial(row_kernel, n_seg, n_tile, leaf), in_spe...  6 us
    pallas_call x8, Pallas kernels, expanded(): pl.pallas_call(functools.partial(expand_kernel, part), in_specs=[in_vmem]...  2.29 us
  transfers between devices with their start and end apart: 25, of which 8 were waited for; matrix products, arithmetic and copies ran while one was open for 0% of the time, Pallas kernels for 27%

profile of v1, /device:TPU:0, one launch (start us, length us, event | category | flops | bytes accessed | tf_op | source)
XLA Modules:
  0.0 60.7 jit_solution(10233893988834106059)
XLA Ops:
  0.0 4.8 %column_side.2 = (f32[512,128]{1,0:T(8,128)S(1)}, f32[512,128]{1,0:T(8,128)S(1)}) custom-call(f32[2048,512]{1,0:T(8,128)} %x_hbm.3, f32[16,64,128]{2,1,0:T(8,128)} %bitcast.12, f32[4,8,128,128]{3,2,1,0:T(8,128)} %bitcast.10, f32[16,64,64]{2,1,0:T(8,128)} %bitcast.14), custom_call_target="tpu_custom_call" | custom-call | flops 1000000 | bytes 100000 | tf_op jit(solution)/shard_map/column_side/pallas_call | solution.py:216
  4.8 0.0 copy-start
  4.8 0.0 copy-start.1
  4.8 3.0 %collective-permute-start = (f32[512,128]{1,0:T(8,128)S(1)}, f32[512,128]{1,0:T(8,128)S(1)}, u32[]{:S(2)}, u32[]{:S(2)}) collective-permute-start(f32[512,128]{1,0:T(8,128)S(1)} %get-tuple-element.61), channel_id=1, source_target_pairs={{0,1},{1,0},{2,3},{3,2},{4,5},{5,4},{6,7},{7,6},{8,9},{9,8},{10,11... | collective-permute-start | bytes 786440 | tf_op jit(solution)/shard_map/ppermute | solution.py:285
  7.8 7.5 %column_side.3 = (f32[512,128]{1,0:T(8,128)S(1)}, f32[512,128]{1,0:T(8,128)S(1)}, f32[512,128]{1,0:T(8,128)S(1)}, f32[512,128]{1,0:T(8,128)S(1)}, f32[512,128]{1,0:T(8,128)S(1)}, /*index=5*/f32[512,128]{1,0:T(8,128)S(1)}) custom-call(f32[2048,512]{1,0:T(8,128)} %x_hbm.3, f32[16,64,128]{2,1,0:T(8,128)} %bitcast.13, f32[4,8,128,128]{3,2,1,0:T(8,128)} %bitcast.11, ...), custom_call_target="tpu_custom_call" | custom-call | flops 1000000 | bytes 100000 | tf_op jit(solution)/shard_map/column_side/pallas_call | solution.py:216
  15.4 0.2 collective-permute-start.4
  15.6 0.2 row_weights.1
  15.8 0.1 collective-permute-start.3
  15.9 0.0 collective-permute-done.refs_1_
  15.9 1.5 %row_side.4 = (f32[256,128]{1,0:T(8,128)S(1)}, f32[256,128]{1,0:T(8,128)S(1)}, f32[256,128]{1,0:T(8,128)S(1)}, f32[256,128]{1,0:T(8,128)S(1)}) custom-call(f32[512,128]{1,0:T(8,128)S(1)} %get-tuple-element.64.refs_0_, f32[512,128]{1,0:T(8,128)S(1)} %collective-permute-done.refs_1_, bf16[4,8,256,128]{3,2,1,0:T(8,128)(2,1)S(1)} %get-tuple-element.66.refs_2_), custom_call_target="tpu_custom_call" | custom-call | flops 20000000000 | bytes 100000 | tf_op jit(solution)/shard_map/row_side/pallas_call | solution.py:262
  17.4 0.6 collective-permute-start.2
  17.9 0.1 collective-permute-start.1
  18.0 1.9 %collective-permute-start.7 = (f32[512,128]{1,0:T(8,128)S(1)}, f32[512,128]{1,0:T(8,128)S(1)}, u32[]{:S(2)}, u32[]{:S(2)}) collective-permute-start(f32[512,128]{1,0:T(8,128)S(1)} %get-tuple-element.83), channel_id=1, source_target_pairs={{0,1},{1,0},{2,3},{3,2},{4,5},{5,4},{6,7},{7,6},{8,9},{9,8},{10,11... | collective-permute-start | bytes 786440 | tf_op jit(solution)/shard_map/ppermute | solution.py:285
  19.9 0.0 collective-permute-done.3.other_ref
  19.9 0.2 expand_weights.1.last_ref
  20.1 0.0 collective-permute-done.2.other_ref
  20.1 0.3 expand.8
  20.4 1.6 %collective-permute-start.5 = (f32[512,128]{1,0:T(8,128)S(1)}, f32[512,128]{1,0:T(8,128)S(1)}, u32[]{:S(2)}, u32[]{:S(2)}) collective-permute-start(f32[512,128]{1,0:T(8,128)S(1)} %expand.8), channel_id=1, source_target_pairs={{0,4},{2,6},{4,0},{6,2},{8,12},{10,14},{12,8},{14,10},{16,20},{18,... | collective-permute-start | bytes 786440 | tf_op jit(solution)/shard_map/ppermute | solution.py:285
  22.0 2.7 %collective-permute-done.4.refs_1_ = f32[512,128]{1,0:T(8,128)S(1)} collective-permute-done((f32[512,128]{1,0:T(8,128)S(1)}, f32[512,128]{1,0:T(8,128)S(1)}, u32[]{:S(2)}, u32[]{:S(2)}) %collective-permute-start.4) | collective-permute-done | bytes 262176 | tf_op jit(solution)/shard_map/ppermute | solution.py:285
  24.7 1.5 %row_side.5 = (f32[256,128]{1,0:T(8,128)S(1)}, f32[256,128]{1,0:T(8,128)S(1)}, f32[256,128]{1,0:T(8,128)S(1)}, f32[256,128]{1,0:T(8,128)S(1)}) custom-call(f32[512,128]{1,0:T(8,128)S(1)} %get-tuple-element.73.refs_0_, f32[512,128]{1,0:T(8,128)S(1)} %collective-permute-done.4.refs_1_, bf16[4,8,256,128]{3,2,1,0:T(8,128)(2,1)S(1)} %get-tuple-element.66.refs_2_), custom_call_target="tpu_custom_call" | custom-call | flops 20000000000 | bytes 100000 | tf_op jit(solution)/shard_map/row_side/pallas_call | solution.py:262
  26.1 0.1 collective-permute-start.6
  26.2 0.5 collective-permute-start.10
  26.7 0.3 expand.9
  27.0 0.5 collective-permute-done.6.other_ref
  27.5 0.3 expand.10
  27.8 1.6 %collective-permute-start.14 = (f32[512,128]{1,0:T(8,128)S(1)}, f32[512,128]{1,0:T(8,128)S(1)}, u32[]{:S(2)}, u32[]{:S(2)}) collective-permute-start(f32[512,128]{1,0:T(8,128)S(1)} %expand.10), channel_id=1, source_target_pairs={{0,4},{2,6},{4,0},{6,2},{8,12},{10,14},{12,8},{14,10},{16,20},{18,... | collective-permute-start | bytes 786440 | tf_op jit(solution)/shard_map/ppermute | solution.py:285
  29.4 0.0 collective-permute-done.7.refs_1_
  29.4 1.6 %row_side.6 = (f32[256,128]{1,0:T(8,128)S(1)}, f32[256,128]{1,0:T(8,128)S(1)}, f32[256,128]{1,0:T(8,128)S(1)}, f32[256,128]{1,0:T(8,128)S(1)}) custom-call(f32[512,128]{1,0:T(8,128)S(1)} %get-tuple-element.81.refs_0_, f32[512,128]{1,0:T(8,128)S(1)} %collective-permute-done.7.refs_1_, bf16[4,8,256,128]{3,2,1,0:T(8,128)(2,1)S(1)} %get-tuple-element.66.refs_2_), custom_call_target="tpu_custom_call" | custom-call | flops 20000000000 | bytes 100000 | tf_op jit(solution)/shard_map/row_side/pallas_call | solution.py:262
  31.1 0.1 collective-permute-start.9
  31.1 0.0 collective-permute-done.10.other_ref
  31.2 0.5 collective-permute-start.13
  31.6 0.3 expand.11
  31.9 0.0 collective-permute-done.5
  32.0 1.6 %collective-permute-start.8 = (f32[256,128]{1,0:T(8,128)S(1)}, f32[256,128]{1,0:T(8,128)S(1)}, u32[]{:S(2)}, u32[]{:S(2)}) collective-permute-start(f32[256,128]{1,0:T(8,128)S(1)} %slice_add_fusion.3), channel_id=1, source_target_pairs={{0,8},{2,10},{4,12},{6,14},{8,0},{10,2},{12,4},{14,6},{16,24},{18,... | collective-permute-start | bytes 393224 | tf_op jit(solution)/shard_map/ppermute | solution.py:285
  33.6 0.3 expand.12
  33.9 1.0 %collective-permute-start.19 = (f32[512,128]{1,0:T(8,128)S(1)}, f32[512,128]{1,0:T(8,128)S(1)}, u32[]{:S(2)}, u32[]{:S(2)}) collective-permute-start(f32[512,128]{1,0:T(8,128)S(1)} %expand.12), channel_id=1, source_target_pairs={{0,4},{2,6},{4,0},{6,2},{8,12},{10,14},{12,8},{14,10},{16,20},{18,... | collective-permute-start | bytes 786440 | tf_op jit(solution)/shard_map/ppermute | solution.py:285
  34.9 0.1 collective-permute-done.11.refs_1_
  35.0 1.5 %row_side.7 = (f32[256,128]{1,0:T(8,128)S(1)}, f32[256,128]{1,0:T(8,128)S(1)}, f32[256,128]{1,0:T(8,128)S(1)}, f32[256,128]{1,0:T(8,128)S(1)}) custom-call(f32[512,128]{1,0:T(8,128)S(1)} %get-tuple-element.92.refs_0_, f32[512,128]{1,0:T(8,128)S(1)} %collective-permute-done.11.refs_1_, bf16[4,8,256,128]{3,2,1,0:T(8,128)(2,1)S(1)} %get-tuple-element.66.refs_2_), custom_call_target="tpu_custom_call" | custom-call | flops 20000000000 | bytes 100000 | tf_op jit(solution)/shard_map/row_side/pallas_call | solution.py:262
  36.5 0.0 collective-permute-done.13.other_ref
  36.5 0.1 collective-permute-start.12
  36.5 0.5 collective-permute-start.16
  37.0 0.3 expand.13
  37.4 1.6 %collective-permute-start.18 = (f32[256,128]{1,0:T(8,128)S(1)}, f32[256,128]{1,0:T(8,128)S(1)}, u32[]{:S(2)}, u32[]{:S(2)}) collective-permute-start(f32[256,128]{1,0:T(8,128)S(1)} %slice_add_fusion.2), channel_id=1, source_target_pairs={{0,8},{2,10},{4,12},{6,14},{8,0},{10,2},{12,4},{14,6},{16,24},{18,... | collective-permute-start | bytes 393224 | tf_op jit(solution)/shard_map/ppermute | solution.py:285
  39.0 0.0 collective-permute-done.12.other_ref
  39.0 0.3 expand.14
  39.3 1.6 %collective-permute-start.17 = (f32[512,128]{1,0:T(8,128)S(1)}, f32[512,128]{1,0:T(8,128)S(1)}, u32[]{:S(2)}, u32[]{:S(2)}) collective-permute-start(f32[512,128]{1,0:T(8,128)S(1)} %expand.14), channel_id=1, source_target_pairs={{0,4},{2,6},{4,0},{6,2},{8,12},{10,14},{12,8},{14,10},{16,20},{18,... | collective-permute-start | bytes 786440 | tf_op jit(solution)/shard_map/ppermute | solution.py:285
  40.9 0.0 collective-permute-done.8
  40.9 0.0 collective-permute-done.16.other_ref
  40.9 2.7 %collective-permute-start.15 = (f32[128,128]{1,0:T(8,128)S(1)}, f32[128,128]{1,0:T(8,128)S(1)}, u32[]{:S(2)}, u32[]{:S(2)}) collective-permute-start(f32[128,128]{1,0:T(8,128)S(1)} %fusion.9), channel_id=1, source_target_pairs={{0,16},{2,18},{4,20},{6,22},{8,24},{10,26},{12,28},{14,30},{16,0},... | collective-permute-start | bytes 196616 | tf_op jit(solution)/shard_map/ppermute | solution.py:285
  43.6 0.3 expand.15
  43.9 0.0 collective-permute-done.19
  43.9 0.5 collective-permute-start.21
  44.4 2.4 %collective-permute-start.22 = (f32[128,128]{1,0:T(8,128)S(1)}, f32[128,128]{1,0:T(8,128)S(1)}, u32[]{:S(2)}, u32[]{:S(2)}) collective-permute-start(f32[128,128]{1,0:T(8,128)S(1)} %fusion.7), channel_id=1, source_target_pairs={{0,16},{2,18},{4,20},{6,22},{8,24},{10,26},{12,28},{14,30},{16,0},... | collective-permute-start | bytes 196616 | tf_op jit(solution)/shard_map/ppermute | solution.py:285
  46.8 0.8 %collective-permute-done.17 = f32[512,128]{1,0:T(8,128)S(1)} collective-permute-done((f32[512,128]{1,0:T(8,128)S(1)}, f32[512,128]{1,0:T(8,128)S(1)}, u32[]{:S(2)}, u32[]{:S(2)}) %collective-permute-start.17) | collective-permute-done | bytes 262176 | tf_op jit(solution)/shard_map/ppermute | solution.py:285
  47.6 1.5 %collective-permute-start.20 = (f32[256,128]{1,0:T(8,128)S(1)}, f32[256,128]{1,0:T(8,128)S(1)}, u32[]{:S(2)}, u32[]{:S(2)}) collective-permute-start(f32[256,128]{1,0:T(8,128)S(1)} %slice_add_fusion), channel_id=1, source_target_pairs={{0,8},{2,10},{4,12},{6,14},{8,0},{10,2},{12,4},{14,6},{16,24},{18,... | collective-permute-start | bytes 393224 | tf_op jit(solution)/shard_map/ppermute | solution.py:285
  49.2 1.9 %collective-permute-done.21 = f32[256,128]{1,0:T(8,128)S(1)} collective-permute-done((f32[256,128]{1,0:T(8,128)S(1)}, f32[256,128]{1,0:T(8,128)S(1)}, u32[]{:S(2)}, u32[]{:S(2)}) %collective-permute-start.21) | collective-permute-done | bytes 131104 | tf_op jit(solution)/shard_map/ppermute | solution.py:285
  51.1 0.8 %collective-permute-start.23 = (f32[128,128]{1,0:T(8,128)S(1)}, f32[128,128]{1,0:T(8,128)S(1)}, u32[]{:S(2)}, u32[]{:S(2)}) collective-permute-start(f32[128,128]{1,0:T(8,128)S(1)} %fusion.6), channel_id=1, source_target_pairs={{0,16},{2,18},{4,20},{6,22},{8,24},{10,26},{12,28},{14,30},{16,0},... | collective-permute-start | bytes 196616 | tf_op jit(solution)/shard_map/ppermute | solution.py:285
  51.8 2.2 %collective-permute-done.20 = f32[256,128]{1,0:T(8,128)S(1)} collective-permute-done((f32[256,128]{1,0:T(8,128)S(1)}, f32[256,128]{1,0:T(8,128)S(1)}, u32[]{:S(2)}, u32[]{:S(2)}) %collective-permute-start.20) | collective-permute-done | bytes 131104 | tf_op jit(solution)/shard_map/ppermute | solution.py:285
  54.1 1.6 %collective-permute-start.24 = (f32[128,128]{1,0:T(8,128)S(1)}, f32[128,128]{1,0:T(8,128)S(1)}, u32[]{:S(2)}, u32[]{:S(2)}) collective-permute-start(f32[128,128]{1,0:T(8,128)S(1)} %fusion.8), channel_id=1, source_target_pairs={{0,16},{2,18},{4,20},{6,22},{8,24},{10,26},{12,28},{14,30},{16,0},... | collective-permute-start | bytes 196616 | tf_op jit(solution)/shard_map/ppermute | solution.py:285
  55.7 0.0 collective-permute-done.22
  55.7 0.0 collective-permute-done.15
  55.8 0.7 %collective-permute-done.23 = f32[128,128]{1,0:T(8,128)S(1)} collective-permute-done((f32[128,128]{1,0:T(8,128)S(1)}, f32[128,128]{1,0:T(8,128)S(1)}, u32[]{:S(2)}, u32[]{:S(2)}) %collective-permute-start.23) | collective-permute-done | bytes 65568 | tf_op jit(solution)/shard_map/ppermute | solution.py:285
  56.5 3.5 %collective-permute-done.24 = f32[128,128]{1,0:T(8,128)S(1)} collective-permute-done((f32[128,128]{1,0:T(8,128)S(1)}, f32[128,128]{1,0:T(8,128)S(1)}, u32[]{:S(2)}, u32[]{:S(2)}) %collective-permute-start.24) | collective-permute-done | bytes 65568 | tf_op jit(solution)/shard_map/ppermute | solution.py:285
  60.0 0.7 %pad_maximum_fusion = f32[128,512]{1,0:T(8,128)} fusion(f32[128,128]{1,0:T(8,128)S(1)} %fusion.1, f32[128,128]{1,0:T(8,128)S(1)} %fusion.3, f32[128,128]{1,0:T(8,128)S(1)} %fusion.5, f32[128,128]{1,0:T(8,128)S(1)} %fusion.11), kind=kLoop, calls=%fused_computation | loop fusion | flops 196608 | bytes 524288 | tf_op jit(solution)/shard_map/concatenate | solution.py:350
  (19 shorter events, 0.2 us)
Async XLA Ops:
  4.8 10.8 %copy-start = (f32[1,16,128,64]{2,3,1,0:T(8,128)S(1)}, f32[1,16,128,64]{2,3,1,0:T(8,128)}, u32[]{:S(2)}) copy-start(f32[1,16,128,64]{2,3,1,0:T(8,128)} %param.11) | copy-start | bytes 1572868
  4.8 10.8 %copy-start.1 = (f32[1,4,8,128,128]{4,3,2,1,0:T(8,128)S(1)}, f32[1,4,8,128,128]{4,3,2,1,0:T(8,128)}, u32[]{:S(2)}) copy-start(f32[1,4,8,128,128]{4,3,2,1,0:T(8,128)} %param.10) | copy-start | bytes 6291460
  4.8 11.1 %collective-permute-start = (f32[512,128]{1,0:T(8,128)S(1)}, f32[512,128]{1,0:T(8,128)S(1)}, u32[]{:S(2)}, u32[]{:S(2)}) collective-permute-start(f32[512,128]{1,0:T(8,128)S(1)} %get-tuple-element.61), channel_id=1, source_target_pairs={{0,1},{1,0},{2,3},{3,2},{4,5},{5,4},{6,7},{7,6},{8,9},{9,8},{10,11... | collective-permute-start | bytes 786440 | tf_op jit(solution)/shard_map/ppermute | solution.py:285
  15.4 9.3 %collective-permute-start.4 = (f32[512,128]{1,0:T(8,128)S(1)}, f32[512,128]{1,0:T(8,128)S(1)}, u32[]{:S(2)}, u32[]{:S(2)}) collective-permute-start(f32[512,128]{1,0:T(8,128)S(1)} %get-tuple-element.74), channel_id=1, source_target_pairs={{0,1},{1,0},{2,3},{3,2},{4,5},{5,4},{6,7},{7,6},{8,9},{9,8},{10,11... | collective-permute-start | bytes 786440 | tf_op jit(solution)/shard_map/ppermute | solution.py:285
  15.8 4.0 %collective-permute-start.3 = (f32[16,64,128]{2,1,0:T(8,128)S(1)}, f32[16,64,128]{2,1,0:T(8,128)S(1)}, u32[]{:S(2)}, u32[]{:S(2)}) collective-permute-start(f32[16,64,128]{2,1,0:T(8,128)S(1)} %get-tuple-element.72), channel_id=1, source_target_pairs={{0,2},{2,0},{4,6},{6,4},{8,10},{10,8},{12,14},{14,12},{16,18},{18,... | collective-permute-start | bytes 1572872 | tf_op jit(solution)/shard_map/ppermute | solution.py:285
  17.4 2.7 %collective-permute-start.2 = (f32[256,128]{1,0:T(8,128)S(1)}, f32[256,128]{1,0:T(8,128)S(1)}, u32[]{:S(2)}, u32[]{:S(2)}) collective-permute-start(f32[256,128]{1,0:T(8,128)S(1)} %get-tuple-element.71), channel_id=1, source_target_pairs={{0,2},{2,0},{4,6},{6,4},{8,10},{10,8},{12,14},{14,12},{16,18},{18,... | collective-permute-start | bytes 393224 | tf_op jit(solution)/shard_map/ppermute | solution.py:285
  17.9 8.2 %collective-permute-start.1 = (f32[256,128]{1,0:T(8,128)S(1)}, f32[256,128]{1,0:T(8,128)S(1)}, u32[]{:S(2)}, u32[]{:S(2)}) collective-permute-start(f32[256,128]{1,0:T(8,128)S(1)} %get-tuple-element.68), channel_id=1, source_target_pairs={{0,2},{2,0},{4,6},{6,4},{8,10},{10,8},{12,14},{14,12},{16,18},{18,... | collective-permute-start | bytes 393224 | tf_op jit(solution)/shard_map/ppermute | solution.py:285
  18.0 11.4 %collective-permute-start.7 = (f32[512,128]{1,0:T(8,128)S(1)}, f32[512,128]{1,0:T(8,128)S(1)}, u32[]{:S(2)}, u32[]{:S(2)}) collective-permute-start(f32[512,128]{1,0:T(8,128)S(1)} %get-tuple-element.83), channel_id=1, source_target_pairs={{0,1},{1,0},{2,3},{3,2},{4,5},{5,4},{6,7},{7,6},{8,9},{9,8},{10,11... | collective-permute-start | bytes 786440 | tf_op jit(solution)/shard_map/ppermute | solution.py:285
  20.4 11.5 %collective-permute-start.5 = (f32[512,128]{1,0:T(8,128)S(1)}, f32[512,128]{1,0:T(8,128)S(1)}, u32[]{:S(2)}, u32[]{:S(2)}) collective-permute-start(f32[512,128]{1,0:T(8,128)S(1)} %expand.8), channel_id=1, source_target_pairs={{0,4},{2,6},{4,0},{6,2},{8,12},{10,14},{12,8},{14,10},{16,20},{18,... | collective-permute-start | bytes 786440 | tf_op jit(solution)/shard_map/ppermute | solution.py:285
  26.1 1.4 %collective-permute-start.6 = (f32[256,128]{1,0:T(8,128)S(1)}, f32[256,128]{1,0:T(8,128)S(1)}, u32[]{:S(2)}, u32[]{:S(2)}) collective-permute-start(f32[256,128]{1,0:T(8,128)S(1)} %get-tuple-element.79), channel_id=1, source_target_pairs={{0,2},{2,0},{4,6},{6,4},{8,10},{10,8},{12,14},{14,12},{16,18},{18,... | collective-permute-start | bytes 393224 | tf_op jit(solution)/shard_map/ppermute | solution.py:285
  26.2 4.9 %collective-permute-start.10 = (f32[256,128]{1,0:T(8,128)S(1)}, f32[256,128]{1,0:T(8,128)S(1)}, u32[]{:S(2)}, u32[]{:S(2)}) collective-permute-start(f32[256,128]{1,0:T(8,128)S(1)} %get-tuple-element.89), channel_id=1, source_target_pairs={{0,2},{2,0},{4,6},{6,4},{8,10},{10,8},{12,14},{14,12},{16,18},{18,... | collective-permute-start | bytes 393224 | tf_op jit(solution)/shard_map/ppermute | solution.py:285
  26.7 8.3 %collective-permute-start.11 = (f32[512,128]{1,0:T(8,128)S(1)}, f32[512,128]{1,0:T(8,128)S(1)}, u32[]{:S(2)}, u32[]{:S(2)}) collective-permute-start(f32[512,128]{1,0:T(8,128)S(1)} %get-tuple-element.94), channel_id=1, source_target_pairs={{0,1},{1,0},{2,3},{3,2},{4,5},{5,4},{6,7},{7,6},{8,9},{9,8},{10,11... | collective-permute-start | bytes 786440 | tf_op jit(solution)/shard_map/ppermute | solution.py:285
  27.8 9.5 %collective-permute-start.14 = (f32[512,128]{1,0:T(8,128)S(1)}, f32[512,128]{1,0:T(8,128)S(1)}, u32[]{:S(2)}, u32[]{:S(2)}) collective-permute-start(f32[512,128]{1,0:T(8,128)S(1)} %expand.10), channel_id=1, source_target_pairs={{0,4},{2,6},{4,0},{6,2},{8,12},{10,14},{12,8},{14,10},{16,20},{18,... | collective-permute-start | bytes 786440 | tf_op jit(solution)/shard_map/ppermute | solution.py:285
  31.1 2.5 %collective-permute-start.9 = (f32[256,128]{1,0:T(8,128)S(1)}, f32[256,128]{1,0:T(8,128)S(1)}, u32[]{:S(2)}, u32[]{:S(2)}) collective-permute-start(f32[256,128]{1,0:T(8,128)S(1)} %get-tuple-element.87), channel_id=1, source_target_pairs={{0,2},{2,0},{4,6},{6,4},{8,10},{10,8},{12,14},{14,12},{16,18},{18,... | collective-permute-start | bytes 393224 | tf_op jit(solution)/shard_map/ppermute | solution.py:285
  31.2 5.3 %collective-permute-start.13 = (f32[256,128]{1,0:T(8,128)S(1)}, f32[256,128]{1,0:T(8,128)S(1)}, u32[]{:S(2)}, u32[]{:S(2)}) collective-permute-start(f32[256,128]{1,0:T(8,128)S(1)} %get-tuple-element.99), channel_id=1, source_target_pairs={{0,2},{2,0},{4,6},{6,4},{8,10},{10,8},{12,14},{14,12},{16,18},{18,... | collective-permute-start | bytes 393224 | tf_op jit(solution)/shard_map/ppermute | solution.py:285
  32.0 8.9 %collective-permute-start.8 = (f32[256,128]{1,0:T(8,128)S(1)}, f32[256,128]{1,0:T(8,128)S(1)}, u32[]{:S(2)}, u32[]{:S(2)}) collective-permute-start(f32[256,128]{1,0:T(8,128)S(1)} %slice_add_fusion.3), channel_id=1, source_target_pairs={{0,8},{2,10},{4,12},{6,14},{8,0},{10,2},{12,4},{14,6},{16,24},{18,... | collective-permute-start | bytes 393224 | tf_op jit(solution)/shard_map/ppermute | solution.py:285
  33.9 10.0 %collective-permute-start.19 = (f32[512,128]{1,0:T(8,128)S(1)}, f32[512,128]{1,0:T(8,128)S(1)}, u32[]{:S(2)}, u32[]{:S(2)}) collective-permute-start(f32[512,128]{1,0:T(8,128)S(1)} %expand.12), channel_id=1, source_target_pairs={{0,4},{2,6},{4,0},{6,2},{8,12},{10,14},{12,8},{14,10},{16,20},{18,... | collective-permute-start | bytes 786440 | tf_op jit(solution)/shard_map/ppermute | solution.py:285
  36.5 2.5 %collective-permute-start.12 = (f32[256,128]{1,0:T(8,128)S(1)}, f32[256,128]{1,0:T(8,128)S(1)}, u32[]{:S(2)}, u32[]{:S(2)}) collective-permute-start(f32[256,128]{1,0:T(8,128)S(1)} %get-tuple-element.97), channel_id=1, source_target_pairs={{0,2},{2,0},{4,6},{6,4},{8,10},{10,8},{12,14},{14,12},{16,18},{18,... | collective-permute-start | bytes 393224 | tf_op jit(solution)/shard_map/ppermute | solution.py:285
  36.5 4.4 %collective-permute-start.16 = (f32[256,128]{1,0:T(8,128)S(1)}, f32[256,128]{1,0:T(8,128)S(1)}, u32[]{:S(2)}, u32[]{:S(2)}) collective-permute-start(f32[256,128]{1,0:T(8,128)S(1)} %get-tuple-element.105), channel_id=1, source_target_pairs={{0,2},{2,0},{4,6},{6,4},{8,10},{10,8},{12,14},{14,12},{16,18},{18,... | collective-permute-start | bytes 393224 | tf_op jit(solution)/shard_map/ppermute | solution.py:285
  37.4 7.1 %collective-permute-start.18 = (f32[256,128]{1,0:T(8,128)S(1)}, f32[256,128]{1,0:T(8,128)S(1)}, u32[]{:S(2)}, u32[]{:S(2)}) collective-permute-start(f32[256,128]{1,0:T(8,128)S(1)} %slice_add_fusion.2), channel_id=1, source_target_pairs={{0,8},{2,10},{4,12},{6,14},{8,0},{10,2},{12,4},{14,6},{16,24},{18,... | collective-permute-start | bytes 393224 | tf_op jit(solution)/shard_map/ppermute | solution.py:285
  39.3 8.3 %collective-permute-start.17 = (f32[512,128]{1,0:T(8,128)S(1)}, f32[512,128]{1,0:T(8,128)S(1)}, u32[]{:S(2)}, u32[]{:S(2)}) collective-permute-start(f32[512,128]{1,0:T(8,128)S(1)} %expand.14), channel_id=1, source_target_pairs={{0,4},{2,6},{4,0},{6,2},{8,12},{10,14},{12,8},{14,10},{16,20},{18,... | collective-permute-start | bytes 786440 | tf_op jit(solution)/shard_map/ppermute | solution.py:285
  40.9 14.8 %collective-permute-start.15 = (f32[128,128]{1,0:T(8,128)S(1)}, f32[128,128]{1,0:T(8,128)S(1)}, u32[]{:S(2)}, u32[]{:S(2)}) collective-permute-start(f32[128,128]{1,0:T(8,128)S(1)} %fusion.9), channel_id=1, source_target_pairs={{0,16},{2,18},{4,20},{6,22},{8,24},{10,26},{12,28},{14,30},{16,0},... | collective-permute-start | bytes 196616 | tf_op jit(solution)/shard_map/ppermute | solution.py:285
  43.9 7.1 %collective-permute-start.21 = (f32[256,128]{1,0:T(8,128)S(1)}, f32[256,128]{1,0:T(8,128)S(1)}, u32[]{:S(2)}, u32[]{:S(2)}) collective-permute-start(f32[256,128]{1,0:T(8,128)S(1)} %slice_add_fusion.1), channel_id=1, source_target_pairs={{0,8},{2,10},{4,12},{6,14},{8,0},{10,2},{12,4},{14,6},{16,24},{18,... | collective-permute-start | bytes 393224 | tf_op jit(solution)/shard_map/ppermute | solution.py:285
  44.4 11.3 %collective-permute-start.22 = (f32[128,128]{1,0:T(8,128)S(1)}, f32[128,128]{1,0:T(8,128)S(1)}, u32[]{:S(2)}, u32[]{:S(2)}) collective-permute-start(f32[128,128]{1,0:T(8,128)S(1)} %fusion.7), channel_id=1, source_target_pairs={{0,16},{2,18},{4,20},{6,22},{8,24},{10,26},{12,28},{14,30},{16,0},... | collective-permute-start | bytes 196616 | tf_op jit(solution)/shard_map/ppermute | solution.py:285
  47.6 6.4 %collective-permute-start.20 = (f32[256,128]{1,0:T(8,128)S(1)}, f32[256,128]{1,0:T(8,128)S(1)}, u32[]{:S(2)}, u32[]{:S(2)}) collective-permute-start(f32[256,128]{1,0:T(8,128)S(1)} %slice_add_fusion), channel_id=1, source_target_pairs={{0,8},{2,10},{4,12},{6,14},{8,0},{10,2},{12,4},{14,6},{16,24},{18,... | collective-permute-start | bytes 393224 | tf_op jit(solution)/shard_map/ppermute | solution.py:285
  51.1 5.4 %collective-permute-start.23 = (f32[128,128]{1,0:T(8,128)S(1)}, f32[128,128]{1,0:T(8,128)S(1)}, u32[]{:S(2)}, u32[]{:S(2)}) collective-permute-start(f32[128,128]{1,0:T(8,128)S(1)} %fusion.6), channel_id=1, source_target_pairs={{0,16},{2,18},{4,20},{6,22},{8,24},{10,26},{12,28},{14,30},{16,0},... | collective-permute-start | bytes 196616 | tf_op jit(solution)/shard_map/ppermute | solution.py:285
  54.1 5.9 %collective-permute-start.24 = (f32[128,128]{1,0:T(8,128)S(1)}, f32[128,128]{1,0:T(8,128)S(1)}, u32[]{:S(2)}, u32[]{:S(2)}) collective-permute-start(f32[128,128]{1,0:T(8,128)S(1)} %fusion.8), channel_id=1, source_target_pairs={{0,16},{2,18},{4,20},{6,22},{8,24},{10,26},{12,28},{14,30},{16,0},... | collective-permute-start | bytes 196616 | tf_op jit(solution)/shard_map/ppermute | solution.py:285

commit v2 on v0

--- a/solution.py
+++ b/solution.py
@@ -29,7 +29,8 @@
 def product3(wide, v_hi, v_lo):
     depth, width = v_hi.shape
     if width > CHUNK:
-        return dot(wide, jnp.concatenate([v_hi, v_hi], axis=0)) + dot(wide[:, :depth], v_lo)
+        deep = jnp.concatenate([wide, wide[:, :depth]], axis=1)
+        return dot(deep, jnp.concatenate([v_hi, v_hi, v_lo], axis=0))
     left = jnp.concatenate([v_hi, v_hi], axis=0)
     right = jnp.concatenate([v_lo, jnp.zeros_like(v_lo)], axis=0)
     both = dot(wide, jnp.concatenate([left, right], axis=1))
@@ -212,7 +213,7 @@
     in_vmem = pl.BlockSpec(memory_space=pltpu.VMEM)
 
     def column_side(start, count, mid, limit):
-        pieces = 4
+        pieces = 8
         width = count * CHUNK
         outs = pl.pallas_call(
             functools.partial(column_kernel, n_seg, pieces, start * CHUNK),

time: 57.4 us -> 58.3 us (1.016)
  Pallas kernels: 16.6 us -> 17.6 us
    pallas_call x2, Pallas kernels: 9.5 us -> 10.4 us  [column_side(): pl.pallas_call(functools.partial(column_kernel, n_seg, pieces, start * CH...]
where the time goes in v2:
time: 58.3 us; the launch traced here: 58.2 us
  starting transfers between devices  27.8 us (48%)
  Pallas kernels  17.6 us (30%)
  waiting for transfers between devices  11.6 us (20%)
  other arithmetic  0.9 us (2%)
    ppermute x25, starting transfers between devices, swap(): return lax.ppermute(x, axis, [(i, i ^ mask) for i in range(size)])  27.8 us
    ppermute x25, waiting for transfers between devices, swap(): return lax.ppermute(x, axis, [(i, i ^ mask) for i in range(size)])  11.6 us
    pallas_call x2, Pallas kernels, column_side(): pl.pallas_call(functools.partial(column_kernel, n_seg, pieces, start * CH...  10.4 us
    pallas_call x4, Pallas kernels, row_side(): pl.pallas_call(functools.partial(row_kernel, n_seg, n_tile, leaf), in_spe...  4.72 us
    pallas_call x8, Pallas kernels, expanded(): pl.pallas_call(functools.partial(expand_kernel, part), in_specs=[in_vmem]...  1.89 us
  transfers between devices with their start and end apart: 25, of which 8 were waited for; matrix products, arithmetic and copies ran while one was open for 0% of the time, Pallas kernels for 23%

profile of v2, /device:TPU:0, one launch (start us, length us, event | category | flops | bytes accessed | tf_op | source)
XLA Modules:
  0.0 58.2 jit_solution(7832763537745655052)
XLA Ops:
  0.0 4.3 %column_side.2 = (f32[512,128]{1,0:T(8,128)S(1)}, f32[512,128]{1,0:T(8,128)S(1)}) custom-call(f32[2048,512]{1,0:T(8,128)} %x_hbm.3, f32[16,64,128]{2,1,0:T(8,128)} %bitcast.12, f32[4,8,128,128]{3,2,1,0:T(8,128)} %bitcast.10, f32[16,64,64]{2,1,0:T(8,128)} %bitcast.14), custom_call_target="tpu_custom_call" | custom-call | flops 1000000 | bytes 100000 | tf_op jit(solution)/shard_map/column_side/pallas_call | solution.py:218
  4.3 0.0 copy-start
  4.3 0.0 copy-start.1
  4.3 3.0 %collective-permute-start = (f32[512,128]{1,0:T(8,128)S(1)}, f32[512,128]{1,0:T(8,128)S(1)}, u32[]{:S(2)}, u32[]{:S(2)}) collective-permute-start(f32[512,128]{1,0:T(8,128)S(1)} %get-tuple-element.61), channel_id=1, source_target_pairs={{0,1},{1,0},{2,3},{3,2},{4,5},{5,4},{6,7},{7,6},{8,9},{9,8},{10,11... | collective-permute-start | bytes 786440 | tf_op jit(solution)/shard_map/ppermute | solution.py:287
  7.3 6.2 %column_side.3 = (f32[512,128]{1,0:T(8,128)S(1)}, f32[512,128]{1,0:T(8,128)S(1)}, f32[512,128]{1,0:T(8,128)S(1)}, f32[512,128]{1,0:T(8,128)S(1)}, f32[512,128]{1,0:T(8,128)S(1)}, /*index=5*/f32[512,128]{1,0:T(8,128)S(1)}) custom-call(f32[2048,512]{1,0:T(8,128)} %x_hbm.3, f32[16,64,128]{2,1,0:T(8,128)} %bitcast.13, f32[4,8,128,128]{3,2,1,0:T(8,128)} %bitcast.11, ...), custom_call_target="tpu_custom_call" | custom-call | flops 1000000 | bytes 100000 | tf_op jit(solution)/shard_map/column_side/pallas_call | solution.py:218
  13.5 0.2 collective-permute-start.4
  13.7 0.3 row_weights.1
  14.0 0.1 collective-permute-start.3
  14.1 0.0 collective-permute-done.refs_1_
  14.1 1.2 %row_side.4 = (f32[256,128]{1,0:T(8,128)S(1)}, f32[256,128]{1,0:T(8,128)S(1)}, f32[256,128]{1,0:T(8,128)S(1)}, f32[256,128]{1,0:T(8,128)S(1)}) custom-call(f32[512,128]{1,0:T(8,128)S(1)} %get-tuple-element.64.refs_0_, f32[512,128]{1,0:T(8,128)S(1)} %collective-permute-done.refs_1_, bf16[4,8,128,256]{3,2,1,0:T(8,128)(2,1)S(1)} %get-tuple-element.66.refs_2_), custom_call_target="tpu_custom_call" | custom-call | flops 20000000000 | bytes 100000 | tf_op jit(solution)/shard_map/row_side/pallas_call | solution.py:264
  15.3 0.5 collective-permute-start.2
  15.8 0.1 collective-permute-start.1
  15.9 1.9 %collective-permute-start.7 = (f32[512,128]{1,0:T(8,128)S(1)}, f32[512,128]{1,0:T(8,128)S(1)}, u32[]{:S(2)}, u32[]{:S(2)}) collective-permute-start(f32[512,128]{1,0:T(8,128)S(1)} %get-tuple-element.83), channel_id=1, source_target_pairs={{0,1},{1,0},{2,3},{3,2},{4,5},{5,4},{6,7},{7,6},{8,9},{9,8},{10,11... | collective-permute-start | bytes 786440 | tf_op jit(solution)/shard_map/ppermute | solution.py:287
  17.8 0.0 collective-permute-done.3.other_ref
  17.8 0.2 expand_weights.1.last_ref
  18.0 0.0 collective-permute-done.2.other_ref
  18.0 0.2 expand.8
  18.3 1.6 %collective-permute-start.5 = (f32[512,128]{1,0:T(8,128)S(1)}, f32[512,128]{1,0:T(8,128)S(1)}, u32[]{:S(2)}, u32[]{:S(2)}) collective-permute-start(f32[512,128]{1,0:T(8,128)S(1)} %expand.8), channel_id=1, source_target_pairs={{0,4},{2,6},{4,0},{6,2},{8,12},{10,14},{12,8},{14,10},{16,20},{18,... | collective-permute-start | bytes 786440 | tf_op jit(solution)/shard_map/ppermute | solution.py:287
  19.8 2.9 %collective-permute-done.4.refs_1_ = f32[512,128]{1,0:T(8,128)S(1)} collective-permute-done((f32[512,128]{1,0:T(8,128)S(1)}, f32[512,128]{1,0:T(8,128)S(1)}, u32[]{:S(2)}, u32[]{:S(2)}) %collective-permute-start.4) | collective-permute-done | bytes 262176 | tf_op jit(solution)/shard_map/ppermute | solution.py:287
  22.8 1.2 %row_side.5 = (f32[256,128]{1,0:T(8,128)S(1)}, f32[256,128]{1,0:T(8,128)S(1)}, f32[256,128]{1,0:T(8,128)S(1)}, f32[256,128]{1,0:T(8,128)S(1)}) custom-call(f32[512,128]{1,0:T(8,128)S(1)} %get-tuple-element.73.refs_0_, f32[512,128]{1,0:T(8,128)S(1)} %collective-permute-done.4.refs_1_, bf16[4,8,128,256]{3,2,1,0:T(8,128)(2,1)S(1)} %get-tuple-element.66.refs_2_), custom_call_target="tpu_custom_call" | custom-call | flops 20000000000 | bytes 100000 | tf_op jit(solution)/shard_map/row_side/pallas_call | solution.py:264
  24.0 0.0 collective-permute-done.1.other_ref
  24.0 0.1 collective-permute-start.6
  24.1 0.5 collective-permute-start.10
  24.6 0.0 collective-permute-start.11
  24.6 0.2 expand.9
  24.8 0.6 %collective-permute-done.6.other_ref = f32[256,128]{1,0:T(8,128)S(1)} collective-permute-done((f32[256,128]{1,0:T(8,128)S(1)}, f32[256,128]{1,0:T(8,128)S(1)}, u32[]{:S(2)}, u32[]{:S(2)}) %collective-permute-start.6) | collective-permute-done | bytes 131104 | tf_op jit(solution)/shard_map/ppermute | solution.py:287
  25.4 0.2 expand.10
  25.6 1.6 %collective-permute-start.14 = (f32[512,128]{1,0:T(8,128)S(1)}, f32[512,128]{1,0:T(8,128)S(1)}, u32[]{:S(2)}, u32[]{:S(2)}) collective-permute-start(f32[512,128]{1,0:T(8,128)S(1)} %expand.10), channel_id=1, source_target_pairs={{0,4},{2,6},{4,0},{6,2},{8,12},{10,14},{12,8},{14,10},{16,20},{18,... | collective-permute-start | bytes 786440 | tf_op jit(solution)/shard_map/ppermute | solution.py:287
  27.2 0.0 collective-permute-done.7.refs_1_
  27.2 1.2 %row_side.6 = (f32[256,128]{1,0:T(8,128)S(1)}, f32[256,128]{1,0:T(8,128)S(1)}, f32[256,128]{1,0:T(8,128)S(1)}, f32[256,128]{1,0:T(8,128)S(1)}) custom-call(f32[512,128]{1,0:T(8,128)S(1)} %get-tuple-element.81.refs_0_, f32[512,128]{1,0:T(8,128)S(1)} %collective-permute-done.7.refs_1_, bf16[4,8,128,256]{3,2,1,0:T(8,128)(2,1)S(1)} %get-tuple-element.66.refs_2_), custom_call_target="tpu_custom_call" | custom-call | flops 20000000000 | bytes 100000 | tf_op jit(solution)/shard_map/row_side/pallas_call | solution.py:264
  28.4 0.1 collective-permute-start.9
  28.5 0.0 collective-permute-done.10.other_ref
  28.5 0.5 collective-permute-start.13
  29.0 0.2 expand.11
  29.2 0.0 collective-permute-done.5
  29.3 1.6 %collective-permute-start.8 = (f32[256,128]{1,0:T(8,128)S(1)}, f32[256,128]{1,0:T(8,128)S(1)}, u32[]{:S(2)}, u32[]{:S(2)}) collective-permute-start(f32[256,128]{1,0:T(8,128)S(1)} %slice_add_fusion.3), channel_id=1, source_target_pairs={{0,8},{2,10},{4,12},{6,14},{8,0},{10,2},{12,4},{14,6},{16,24},{18,... | collective-permute-start | bytes 393224 | tf_op jit(solution)/shard_map/ppermute | solution.py:287
  30.9 0.0 collective-permute-done.9.other_ref
  30.9 0.2 expand.12
  31.2 1.3 %collective-permute-start.19 = (f32[512,128]{1,0:T(8,128)S(1)}, f32[512,128]{1,0:T(8,128)S(1)}, u32[]{:S(2)}, u32[]{:S(2)}) collective-permute-start(f32[512,128]{1,0:T(8,128)S(1)} %expand.12), channel_id=1, source_target_pairs={{0,4},{2,6},{4,0},{6,2},{8,12},{10,14},{12,8},{14,10},{16,20},{18,... | collective-permute-start | bytes 786440 | tf_op jit(solution)/shard_map/ppermute | solution.py:287
  32.5 0.4 collective-permute-done.11.refs_1_
  32.8 1.2 %row_side.7 = (f32[256,128]{1,0:T(8,128)S(1)}, f32[256,128]{1,0:T(8,128)S(1)}, f32[256,128]{1,0:T(8,128)S(1)}, f32[256,128]{1,0:T(8,128)S(1)}) custom-call(f32[512,128]{1,0:T(8,128)S(1)} %get-tuple-element.92.refs_0_, f32[512,128]{1,0:T(8,128)S(1)} %collective-permute-done.11.refs_1_, bf16[4,8,128,256]{3,2,1,0:T(8,128)(2,1)S(1)} %get-tuple-element.66.refs_2_), custom_call_target="tpu_custom_call" | custom-call | flops 20000000000 | bytes 100000 | tf_op jit(solution)/shard_map/row_side/pallas_call | solution.py:264
  34.0 0.1 collective-permute-start.12
  34.1 0.5 collective-permute-start.16
  34.6 0.2 expand.13
  34.9 1.6 %collective-permute-start.18 = (f32[256,128]{1,0:T(8,128)S(1)}, f32[256,128]{1,0:T(8,128)S(1)}, u32[]{:S(2)}, u32[]{:S(2)}) collective-permute-start(f32[256,128]{1,0:T(8,128)S(1)} %slice_add_fusion.2), channel_id=1, source_target_pairs={{0,8},{2,10},{4,12},{6,14},{8,0},{10,2},{12,4},{14,6},{16,24},{18,... | collective-permute-start | bytes 393224 | tf_op jit(solution)/shard_map/ppermute | solution.py:287
  36.6 0.2 expand.14
  36.8 1.6 %collective-permute-start.17 = (f32[512,128]{1,0:T(8,128)S(1)}, f32[512,128]{1,0:T(8,128)S(1)}, u32[]{:S(2)}, u32[]{:S(2)}) collective-permute-start(f32[512,128]{1,0:T(8,128)S(1)} %expand.14), channel_id=1, source_target_pairs={{0,4},{2,6},{4,0},{6,2},{8,12},{10,14},{12,8},{14,10},{16,20},{18,... | collective-permute-start | bytes 786440 | tf_op jit(solution)/shard_map/ppermute | solution.py:287
  38.4 0.0 collective-permute-done.8
  38.4 2.7 %collective-permute-start.15 = (f32[128,128]{1,0:T(8,128)S(1)}, f32[128,128]{1,0:T(8,128)S(1)}, u32[]{:S(2)}, u32[]{:S(2)}) collective-permute-start(f32[128,128]{1,0:T(8,128)S(1)} %fusion.9), channel_id=1, source_target_pairs={{0,16},{2,18},{4,20},{6,22},{8,24},{10,26},{12,28},{14,30},{16,0},... | collective-permute-start | bytes 196616 | tf_op jit(solution)/shard_map/ppermute | solution.py:287
  41.1 0.2 expand.15
  41.3 0.0 collective-permute-done.19
  41.3 0.8 %collective-permute-start.21 = (f32[256,128]{1,0:T(8,128)S(1)}, f32[256,128]{1,0:T(8,128)S(1)}, u32[]{:S(2)}, u32[]{:S(2)}) collective-permute-start(f32[256,128]{1,0:T(8,128)S(1)} %slice_add_fusion.1), channel_id=1, source_target_pairs={{0,8},{2,10},{4,12},{6,14},{8,0},{10,2},{12,4},{14,6},{16,24},{18,... | collective-permute-start | bytes 393224 | tf_op jit(solution)/shard_map/ppermute | solution.py:287
  42.2 2.7 %collective-permute-start.22 = (f32[128,128]{1,0:T(8,128)S(1)}, f32[128,128]{1,0:T(8,128)S(1)}, u32[]{:S(2)}, u32[]{:S(2)}) collective-permute-start(f32[128,128]{1,0:T(8,128)S(1)} %fusion.7), channel_id=1, source_target_pairs={{0,16},{2,18},{4,20},{6,22},{8,24},{10,26},{12,28},{14,30},{16,0},... | collective-permute-start | bytes 196616 | tf_op jit(solution)/shard_map/ppermute | solution.py:287
  44.8 0.5 collective-permute-done.17
  45.3 1.6 %collective-permute-start.20 = (f32[256,128]{1,0:T(8,128)S(1)}, f32[256,128]{1,0:T(8,128)S(1)}, u32[]{:S(2)}, u32[]{:S(2)}) collective-permute-start(f32[256,128]{1,0:T(8,128)S(1)} %slice_add_fusion), channel_id=1, source_target_pairs={{0,8},{2,10},{4,12},{6,14},{8,0},{10,2},{12,4},{14,6},{16,24},{18,... | collective-permute-start | bytes 393224 | tf_op jit(solution)/shard_map/ppermute | solution.py:287
  47.0 1.4 %collective-permute-done.21 = f32[256,128]{1,0:T(8,128)S(1)} collective-permute-done((f32[256,128]{1,0:T(8,128)S(1)}, f32[256,128]{1,0:T(8,128)S(1)}, u32[]{:S(2)}, u32[]{:S(2)}) %collective-permute-start.21) | collective-permute-done | bytes 131104 | tf_op jit(solution)/shard_map/ppermute | solution.py:287
  48.4 1.2 %collective-permute-start.23 = (f32[128,128]{1,0:T(8,128)S(1)}, f32[128,128]{1,0:T(8,128)S(1)}, u32[]{:S(2)}, u32[]{:S(2)}) collective-permute-start(f32[128,128]{1,0:T(8,128)S(1)} %fusion.6), channel_id=1, source_target_pairs={{0,16},{2,18},{4,20},{6,22},{8,24},{10,26},{12,28},{14,30},{16,0},... | collective-permute-start | bytes 196616 | tf_op jit(solution)/shard_map/ppermute | solution.py:287
  49.6 1.8 %collective-permute-done.20 = f32[256,128]{1,0:T(8,128)S(1)} collective-permute-done((f32[256,128]{1,0:T(8,128)S(1)}, f32[256,128]{1,0:T(8,128)S(1)}, u32[]{:S(2)}, u32[]{:S(2)}) %collective-permute-start.20) | collective-permute-done | bytes 131104 | tf_op jit(solution)/shard_map/ppermute | solution.py:287
  51.5 2.0 %collective-permute-start.24 = (f32[128,128]{1,0:T(8,128)S(1)}, f32[128,128]{1,0:T(8,128)S(1)}, u32[]{:S(2)}, u32[]{:S(2)}) collective-permute-start(f32[128,128]{1,0:T(8,128)S(1)} %fusion.8), channel_id=1, source_target_pairs={{0,16},{2,18},{4,20},{6,22},{8,24},{10,26},{12,28},{14,30},{16,0},... | collective-permute-start | bytes 196616 | tf_op jit(solution)/shard_map/ppermute | solution.py:287
  53.5 0.0 collective-permute-done.22
  53.5 0.0 collective-permute-done.15
  53.6 2.1 %collective-permute-done.23 = f32[128,128]{1,0:T(8,128)S(1)} collective-permute-done((f32[128,128]{1,0:T(8,128)S(1)}, f32[128,128]{1,0:T(8,128)S(1)}, u32[]{:S(2)}, u32[]{:S(2)}) %collective-permute-start.23) | collective-permute-done | bytes 65568 | tf_op jit(solution)/shard_map/ppermute | solution.py:287
  55.6 1.8 %collective-permute-done.24 = f32[128,128]{1,0:T(8,128)S(1)} collective-permute-done((f32[128,128]{1,0:T(8,128)S(1)}, f32[128,128]{1,0:T(8,128)S(1)}, u32[]{:S(2)}, u32[]{:S(2)}) %collective-permute-start.24) | collective-permute-done | bytes 65568 | tf_op jit(solution)/shard_map/ppermute | solution.py:287
  57.5 0.7 %pad_maximum_fusion = f32[128,512]{1,0:T(8,128)} fusion(f32[128,128]{1,0:T(8,128)S(1)} %fusion.1, f32[128,128]{1,0:T(8,128)S(1)} %fusion.3, f32[128,128]{1,0:T(8,128)S(1)} %fusion.5, f32[128,128]{1,0:T(8,128)S(1)} %fusion.11), kind=kLoop, calls=%fused_computation | loop fusion | flops 196608 | bytes 524288 | tf_op jit(solution)/shard_map/concatenate | solution.py:352
  (19 shorter events, 0.2 us)
Async XLA Ops:
  4.3 9.4 %copy-start = (f32[1,16,128,64]{2,3,1,0:T(8,128)S(1)}, f32[1,16,128,64]{2,3,1,0:T(8,128)}, u32[]{:S(2)}) copy-start(f32[1,16,128,64]{2,3,1,0:T(8,128)} %param.11) | copy-start | bytes 1572868
  4.3 9.4 %copy-start.1 = (f32[1,4,8,128,128]{4,3,2,1,0:T(8,128)S(1)}, f32[1,4,8,128,128]{4,3,2,1,0:T(8,128)}, u32[]{:S(2)}) copy-start(f32[1,4,8,128,128]{4,3,2,1,0:T(8,128)} %param.10) | copy-start | bytes 6291460
  4.3 9.8 %collective-permute-start = (f32[512,128]{1,0:T(8,128)S(1)}, f32[512,128]{1,0:T(8,128)S(1)}, u32[]{:S(2)}, u32[]{:S(2)}) collective-permute-start(f32[512,128]{1,0:T(8,128)S(1)} %get-tuple-element.61), channel_id=1, source_target_pairs={{0,1},{1,0},{2,3},{3,2},{4,5},{5,4},{6,7},{7,6},{8,9},{9,8},{10,11... | collective-permute-start | bytes 786440 | tf_op jit(solution)/shard_map/ppermute | solution.py:287
  13.5 9.3 %collective-permute-start.4 = (f32[512,128]{1,0:T(8,128)S(1)}, f32[512,128]{1,0:T(8,128)S(1)}, u32[]{:S(2)}, u32[]{:S(2)}) collective-permute-start(f32[512,128]{1,0:T(8,128)S(1)} %get-tuple-element.74), channel_id=1, source_target_pairs={{0,1},{1,0},{2,3},{3,2},{4,5},{5,4},{6,7},{7,6},{8,9},{9,8},{10,11... | collective-permute-start | bytes 786440 | tf_op jit(solution)/shard_map/ppermute | solution.py:287
  14.0 3.8 %collective-permute-start.3 = (f32[16,64,128]{2,1,0:T(8,128)S(1)}, f32[16,64,128]{2,1,0:T(8,128)S(1)}, u32[]{:S(2)}, u32[]{:S(2)}) collective-permute-start(f32[16,64,128]{2,1,0:T(8,128)S(1)} %get-tuple-element.72), channel_id=1, source_target_pairs={{0,2},{2,0},{4,6},{6,4},{8,10},{10,8},{12,14},{14,12},{16,18},{18,... | collective-permute-start | bytes 1572872 | tf_op jit(solution)/shard_map/ppermute | solution.py:287
  15.3 2.7 %collective-permute-start.2 = (f32[256,128]{1,0:T(8,128)S(1)}, f32[256,128]{1,0:T(8,128)S(1)}, u32[]{:S(2)}, u32[]{:S(2)}) collective-permute-start(f32[256,128]{1,0:T(8,128)S(1)} %get-tuple-element.71), channel_id=1, source_target_pairs={{0,2},{2,0},{4,6},{6,4},{8,10},{10,8},{12,14},{14,12},{16,18},{18,... | collective-permute-start | bytes 393224 | tf_op jit(solution)/shard_map/ppermute | solution.py:287
  15.8 8.1 %collective-permute-start.1 = (f32[256,128]{1,0:T(8,128)S(1)}, f32[256,128]{1,0:T(8,128)S(1)}, u32[]{:S(2)}, u32[]{:S(2)}) collective-permute-start(f32[256,128]{1,0:T(8,128)S(1)} %get-tuple-element.68), channel_id=1, source_target_pairs={{0,2},{2,0},{4,6},{6,4},{8,10},{10,8},{12,14},{14,12},{16,18},{18,... | collective-permute-start | bytes 393224 | tf_op jit(solution)/shard_map/ppermute | solution.py:287
  15.9 11.3 %collective-permute-start.7 = (f32[512,128]{1,0:T(8,128)S(1)}, f32[512,128]{1,0:T(8,128)S(1)}, u32[]{:S(2)}, u32[]{:S(2)}) collective-permute-start(f32[512,128]{1,0:T(8,128)S(1)} %get-tuple-element.83), channel_id=1, source_target_pairs={{0,1},{1,0},{2,3},{3,2},{4,5},{5,4},{6,7},{7,6},{8,9},{9,8},{10,11... | collective-permute-start | bytes 786440 | tf_op jit(solution)/shard_map/ppermute | solution.py:287
  18.3 11.0 %collective-permute-start.5 = (f32[512,128]{1,0:T(8,128)S(1)}, f32[512,128]{1,0:T(8,128)S(1)}, u32[]{:S(2)}, u32[]{:S(2)}) collective-permute-start(f32[512,128]{1,0:T(8,128)S(1)} %expand.8), channel_id=1, source_target_pairs={{0,4},{2,6},{4,0},{6,2},{8,12},{10,14},{12,8},{14,10},{16,20},{18,... | collective-permute-start | bytes 786440 | tf_op jit(solution)/shard_map/ppermute | solution.py:287
  24.0 1.4 %collective-permute-start.6 = (f32[256,128]{1,0:T(8,128)S(1)}, f32[256,128]{1,0:T(8,128)S(1)}, u32[]{:S(2)}, u32[]{:S(2)}) collective-permute-start(f32[256,128]{1,0:T(8,128)S(1)} %get-tuple-element.79), channel_id=1, source_target_pairs={{0,2},{2,0},{4,6},{6,4},{8,10},{10,8},{12,14},{14,12},{16,18},{18,... | collective-permute-start | bytes 393224 | tf_op jit(solution)/shard_map/ppermute | solution.py:287
  24.1 4.4 %collective-permute-start.10 = (f32[256,128]{1,0:T(8,128)S(1)}, f32[256,128]{1,0:T(8,128)S(1)}, u32[]{:S(2)}, u32[]{:S(2)}) collective-permute-start(f32[256,128]{1,0:T(8,128)S(1)} %get-tuple-element.89), channel_id=1, source_target_pairs={{0,2},{2,0},{4,6},{6,4},{8,10},{10,8},{12,14},{14,12},{16,18},{18,... | collective-permute-start | bytes 393224 | tf_op jit(solution)/shard_map/ppermute | solution.py:287
  24.6 8.3 %collective-permute-start.11 = (f32[512,128]{1,0:T(8,128)S(1)}, f32[512,128]{1,0:T(8,128)S(1)}, u32[]{:S(2)}, u32[]{:S(2)}) collective-permute-start(f32[512,128]{1,0:T(8,128)S(1)} %get-tuple-element.94), channel_id=1, source_target_pairs={{0,1},{1,0},{2,3},{3,2},{4,5},{5,4},{6,7},{7,6},{8,9},{9,8},{10,11... | collective-permute-start | bytes 786440 | tf_op jit(solution)/shard_map/ppermute | solution.py:287
  25.6 9.2 %collective-permute-start.14 = (f32[512,128]{1,0:T(8,128)S(1)}, f32[512,128]{1,0:T(8,128)S(1)}, u32[]{:S(2)}, u32[]{:S(2)}) collective-permute-start(f32[512,128]{1,0:T(8,128)S(1)} %expand.10), channel_id=1, source_target_pairs={{0,4},{2,6},{4,0},{6,2},{8,12},{10,14},{12,8},{14,10},{16,20},{18,... | collective-permute-start | bytes 786440 | tf_op jit(solution)/shard_map/ppermute | solution.py:287
  28.4 2.5 %collective-permute-start.9 = (f32[256,128]{1,0:T(8,128)S(1)}, f32[256,128]{1,0:T(8,128)S(1)}, u32[]{:S(2)}, u32[]{:S(2)}) collective-permute-start(f32[256,128]{1,0:T(8,128)S(1)} %get-tuple-element.87), channel_id=1, source_target_pairs={{0,2},{2,0},{4,6},{6,4},{8,10},{10,8},{12,14},{14,12},{16,18},{18,... | collective-permute-start | bytes 393224 | tf_op jit(solution)/shard_map/ppermute | solution.py:287
  28.5 5.5 %collective-permute-start.13 = (f32[256,128]{1,0:T(8,128)S(1)}, f32[256,128]{1,0:T(8,128)S(1)}, u32[]{:S(2)}, u32[]{:S(2)}) collective-permute-start(f32[256,128]{1,0:T(8,128)S(1)} %get-tuple-element.99), channel_id=1, source_target_pairs={{0,2},{2,0},{4,6},{6,4},{8,10},{10,8},{12,14},{14,12},{16,18},{18,... | collective-permute-start | bytes 393224 | tf_op jit(solution)/shard_map/ppermute | solution.py:287
  29.3 9.1 %collective-permute-start.8 = (f32[256,128]{1,0:T(8,128)S(1)}, f32[256,128]{1,0:T(8,128)S(1)}, u32[]{:S(2)}, u32[]{:S(2)}) collective-permute-start(f32[256,128]{1,0:T(8,128)S(1)} %slice_add_fusion.3), channel_id=1, source_target_pairs={{0,8},{2,10},{4,12},{6,14},{8,0},{10,2},{12,4},{14,6},{16,24},{18,... | collective-permute-start | bytes 393224 | tf_op jit(solution)/shard_map/ppermute | solution.py:287
  31.2 10.1 %collective-permute-start.19 = (f32[512,128]{1,0:T(8,128)S(1)}, f32[512,128]{1,0:T(8,128)S(1)}, u32[]{:S(2)}, u32[]{:S(2)}) collective-permute-start(f32[512,128]{1,0:T(8,128)S(1)} %expand.12), channel_id=1, source_target_pairs={{0,4},{2,6},{4,0},{6,2},{8,12},{10,14},{12,8},{14,10},{16,20},{18,... | collective-permute-start | bytes 786440 | tf_op jit(solution)/shard_map/ppermute | solution.py:287
  34.0 2.5 %collective-permute-start.12 = (f32[256,128]{1,0:T(8,128)S(1)}, f32[256,128]{1,0:T(8,128)S(1)}, u32[]{:S(2)}, u32[]{:S(2)}) collective-permute-start(f32[256,128]{1,0:T(8,128)S(1)} %get-tuple-element.97), channel_id=1, source_target_pairs={{0,2},{2,0},{4,6},{6,4},{8,10},{10,8},{12,14},{14,12},{16,18},{18,... | collective-permute-start | bytes 393224 | tf_op jit(solution)/shard_map/ppermute | solution.py:287
  34.1 4.3 %collective-permute-start.16 = (f32[256,128]{1,0:T(8,128)S(1)}, f32[256,128]{1,0:T(8,128)S(1)}, u32[]{:S(2)}, u32[]{:S(2)}) collective-permute-start(f32[256,128]{1,0:T(8,128)S(1)} %get-tuple-element.105), channel_id=1, source_target_pairs={{0,2},{2,0},{4,6},{6,4},{8,10},{10,8},{12,14},{14,12},{16,18},{18,... | collective-permute-start | bytes 393224 | tf_op jit(solution)/shard_map/ppermute | solution.py:287
  34.9 7.2 %collective-permute-start.18 = (f32[256,128]{1,0:T(8,128)S(1)}, f32[256,128]{1,0:T(8,128)S(1)}, u32[]{:S(2)}, u32[]{:S(2)}) collective-permute-start(f32[256,128]{1,0:T(8,128)S(1)} %slice_add_fusion.2), channel_id=1, source_target_pairs={{0,8},{2,10},{4,12},{6,14},{8,0},{10,2},{12,4},{14,6},{16,24},{18,... | collective-permute-start | bytes 393224 | tf_op jit(solution)/shard_map/ppermute | solution.py:287
  36.8 8.5 %collective-permute-start.17 = (f32[512,128]{1,0:T(8,128)S(1)}, f32[512,128]{1,0:T(8,128)S(1)}, u32[]{:S(2)}, u32[]{:S(2)}) collective-permute-start(f32[512,128]{1,0:T(8,128)S(1)} %expand.14), channel_id=1, source_target_pairs={{0,4},{2,6},{4,0},{6,2},{8,12},{10,14},{12,8},{14,10},{16,20},{18,... | collective-permute-start | bytes 786440 | tf_op jit(solution)/shard_map/ppermute | solution.py:287
  38.4 15.1 %collective-permute-start.15 = (f32[128,128]{1,0:T(8,128)S(1)}, f32[128,128]{1,0:T(8,128)S(1)}, u32[]{:S(2)}, u32[]{:S(2)}) collective-permute-start(f32[128,128]{1,0:T(8,128)S(1)} %fusion.9), channel_id=1, source_target_pairs={{0,16},{2,18},{4,20},{6,22},{8,24},{10,26},{12,28},{14,30},{16,0},... | collective-permute-start | bytes 196616 | tf_op jit(solution)/shard_map/ppermute | solution.py:287
  41.3 7.1 %collective-permute-start.21 = (f32[256,128]{1,0:T(8,128)S(1)}, f32[256,128]{1,0:T(8,128)S(1)}, u32[]{:S(2)}, u32[]{:S(2)}) collective-permute-start(f32[256,128]{1,0:T(8,128)S(1)} %slice_add_fusion.1), channel_id=1, source_target_pairs={{0,8},{2,10},{4,12},{6,14},{8,0},{10,2},{12,4},{14,6},{16,24},{18,... | collective-permute-start | bytes 393224 | tf_op jit(solution)/shard_map/ppermute | solution.py:287
  42.2 11.4 %collective-permute-start.22 = (f32[128,128]{1,0:T(8,128)S(1)}, f32[128,128]{1,0:T(8,128)S(1)}, u32[]{:S(2)}, u32[]{:S(2)}) collective-permute-start(f32[128,128]{1,0:T(8,128)S(1)} %fusion.7), channel_id=1, source_target_pairs={{0,16},{2,18},{4,20},{6,22},{8,24},{10,26},{12,28},{14,30},{16,0},... | collective-permute-start | bytes 196616 | tf_op jit(solution)/shard_map/ppermute | solution.py:287
  45.3 6.2 %collective-permute-start.20 = (f32[256,128]{1,0:T(8,128)S(1)}, f32[256,128]{1,0:T(8,128)S(1)}, u32[]{:S(2)}, u32[]{:S(2)}) collective-permute-start(f32[256,128]{1,0:T(8,128)S(1)} %slice_add_fusion), channel_id=1, source_target_pairs={{0,8},{2,10},{4,12},{6,14},{8,0},{10,2},{12,4},{14,6},{16,24},{18,... | collective-permute-start | bytes 393224 | tf_op jit(solution)/shard_map/ppermute | solution.py:287
  48.4 7.2 %collective-permute-start.23 = (f32[128,128]{1,0:T(8,128)S(1)}, f32[128,128]{1,0:T(8,128)S(1)}, u32[]{:S(2)}, u32[]{:S(2)}) collective-permute-start(f32[128,128]{1,0:T(8,128)S(1)} %fusion.6), channel_id=1, source_target_pairs={{0,16},{2,18},{4,20},{6,22},{8,24},{10,26},{12,28},{14,30},{16,0},... | collective-permute-start | bytes 196616 | tf_op jit(solution)/shard_map/ppermute | solution.py:287
  51.5 5.9 %collective-permute-start.24 = (f32[128,128]{1,0:T(8,128)S(1)}, f32[128,128]{1,0:T(8,128)S(1)}, u32[]{:S(2)}, u32[]{:S(2)}) collective-permute-start(f32[128,128]{1,0:T(8,128)S(1)} %fusion.8), channel_id=1, source_target_pairs={{0,16},{2,18},{4,20},{6,22},{8,24},{10,26},{12,28},{14,30},{16,0},... | collective-permute-start | bytes 196616 | tf_op jit(solution)/shard_map/ppermute | solution.py:287

commit v3 on v2

--- a/solution.py
+++ b/solution.py
@@ -86,7 +86,7 @@
 def column_kernel(n_seg, pieces, start, x_hbm, proj_hbm, col_hbm, mid_hbm, *refs):
     outs, (x_ref, proj_ref, col_ref, mid_ref, hi, lo, sems) = refs[:-7], refs[-7:]
     box, rank, leaf = proj_ref.shape
-    levels, pairs = col_ref.shape[:2]
+    levels = col_ref.shape[0]
     width = x_ref.shape[1]
     per = box // pieces
     copies = []
@@ -104,8 +104,7 @@
             fetch(proj_hbm.at[leaves], proj_ref.at[leaves]),
             fetch(x_hbm.at[rows, pl.ds(start, width)], x_ref.at[rows, :]),
         ))
-    halves = [pl.ds(k * (pairs // 2), pairs // 2) for k in range(2)]
-    cols = [[fetch(col_hbm.at[k, h], col_ref.at[k, h]) for h in halves] for k in range(levels)]
+    cols = [fetch(col_hbm.at[k], col_ref.at[k]) for k in range(levels)]
     mid = fetch(mid_hbm, mid_ref)
 
     cuts = cuts_of(width)
@@ -115,8 +114,7 @@
         for n in range(k * per, (k + 1) * per):
             project(n, wide_of(proj_ref[n]), x_ref, hi, lo, cuts)
     for level in range(levels):
-        for copy in cols[level]:
-            copy.wait()
+        cols[level].wait()
         level_step(level, lambda j: wide_of(col_ref[level, j]), hi, lo, rank, cuts)
     mid.wait()
     middle(n_seg, mid_ref, outs, hi, lo, cuts)
@@ -213,7 +211,7 @@
     in_vmem = pl.BlockSpec(memory_space=pltpu.VMEM)
 
     def column_side(start, count, mid, limit):
-        pieces = 8
+        pieces = 2
         width = count * CHUNK
         outs = pl.pallas_call(
             functools.partial(column_kernel, n_seg, pieces, start * CHUNK),
@@ -227,7 +225,7 @@
                 pltpu.VMEM(mid.shape, F32),
                 pltpu.VMEM((box * rank, width), BF16),
                 pltpu.VMEM((box * rank, width), BF16),
-                pltpu.SemaphoreType.DMA((2 * pieces + 2 * levels + 1,)),
+                pltpu.SemaphoreType.DMA((2 * pieces + levels + 1,)),
             ],
             compiler_params=pltpu.CompilerParams(vmem_limit_bytes=limit * 2**20),
             cost_estimate=cost,

time: 58.3 us -> 57 us (0.978)
  Pallas kernels: 17.6 us -> 16.2 us
    pallas_call x2, Pallas kernels: 10.4 us -> 9.1 us  [column_side(): pl.pallas_call(functools.partial(column_kernel, n_seg, pieces, start * CH...]
  transfers between devices with their start and end apart: 25 -> 25, of which waited for: 8 -> 8; matrix products, arithmetic and copies ran while one was open for 0% -> 0% of each run, Pallas kernels for 23% -> 22%
where the time goes in v3:
time: 57 us; the launch traced here: 56.8 us
  starting transfers between devices  27.8 us (49%)
  Pallas kernels  16.2 us (28%)
  waiting for transfers between devices  11.6 us (20%)
  other arithmetic  0.9 us (2%)
    ppermute x25, starting transfers between devices, swap(): return lax.ppermute(x, axis, [(i, i ^ mask) for i in range(size)])  27.8 us
    ppermute x25, waiting for transfers between devices, swap(): return lax.ppermute(x, axis, [(i, i ^ mask) for i in range(size)])  11.6 us
    pallas_call x2, Pallas kernels, column_side(): pl.pallas_call(functools.partial(column_kernel, n_seg, pieces, start * CH...  9.1 us
    pallas_call x4, Pallas kernels, row_side(): pl.pallas_call(functools.partial(row_kernel, n_seg, n_tile, leaf), in_spe...  4.72 us
    pallas_call x8, Pallas kernels, expanded(): pl.pallas_call(functools.partial(expand_kernel, part), in_specs=[in_vmem]...  1.89 us
  transfers between devices with their start and end apart: 25, of which 8 were waited for; matrix products, arithmetic and copies ran while one was open for 0% of the time, Pallas kernels for 22%

profile of v3, /device:TPU:0, one launch (start us, length us, event | category | flops | bytes accessed | tf_op | source)
XLA Modules:
  0.0 56.8 jit_solution(12538062184577015365)
XLA Ops:
  0.0 3.4 %column_side.2 = (f32[512,128]{1,0:T(8,128)S(1)}, f32[512,128]{1,0:T(8,128)S(1)}) custom-call(f32[2048,512]{1,0:T(8,128)} %x_hbm.3, f32[16,64,128]{2,1,0:T(8,128)} %bitcast.12, f32[4,8,128,128]{3,2,1,0:T(8,128)} %bitcast.10, f32[16,64,64]{2,1,0:T(8,128)} %bitcast.14), custom_call_target="tpu_custom_call" | custom-call | flops 1000000 | bytes 100000 | tf_op jit(solution)/shard_map/column_side/pallas_call | solution.py:216
  3.5 0.0 copy-start
  3.5 0.0 copy-start.1
  3.5 3.0 %collective-permute-start = (f32[512,128]{1,0:T(8,128)S(1)}, f32[512,128]{1,0:T(8,128)S(1)}, u32[]{:S(2)}, u32[]{:S(2)}) collective-permute-start(f32[512,128]{1,0:T(8,128)S(1)} %get-tuple-element.61), channel_id=1, source_target_pairs={{0,1},{1,0},{2,3},{3,2},{4,5},{5,4},{6,7},{7,6},{8,9},{9,8},{10,11... | collective-permute-start | bytes 786440 | tf_op jit(solution)/shard_map/ppermute | solution.py:285
  6.5 5.7 %column_side.3 = (f32[512,128]{1,0:T(8,128)S(1)}, f32[512,128]{1,0:T(8,128)S(1)}, f32[512,128]{1,0:T(8,128)S(1)}, f32[512,128]{1,0:T(8,128)S(1)}, f32[512,128]{1,0:T(8,128)S(1)}, /*index=5*/f32[512,128]{1,0:T(8,128)S(1)}) custom-call(f32[2048,512]{1,0:T(8,128)} %x_hbm.3, f32[16,64,128]{2,1,0:T(8,128)} %bitcast.13, f32[4,8,128,128]{3,2,1,0:T(8,128)} %bitcast.11, ...), custom_call_target="tpu_custom_call" | custom-call | flops 1000000 | bytes 100000 | tf_op jit(solution)/shard_map/column_side/pallas_call | solution.py:216
  12.1 0.2 collective-permute-start.4
  12.4 0.3 row_weights.1
  12.7 0.1 collective-permute-start.3
  12.8 0.0 collective-permute-done.refs_1_
  12.8 1.2 %row_side.4 = (f32[256,128]{1,0:T(8,128)S(1)}, f32[256,128]{1,0:T(8,128)S(1)}, f32[256,128]{1,0:T(8,128)S(1)}, f32[256,128]{1,0:T(8,128)S(1)}) custom-call(f32[512,128]{1,0:T(8,128)S(1)} %get-tuple-element.64.refs_0_, f32[512,128]{1,0:T(8,128)S(1)} %collective-permute-done.refs_1_, bf16[4,8,128,256]{3,2,1,0:T(8,128)(2,1)S(1)} %get-tuple-element.66.refs_2_), custom_call_target="tpu_custom_call" | custom-call | flops 20000000000 | bytes 100000 | tf_op jit(solution)/shard_map/row_side/pallas_call | solution.py:262
  14.0 0.5 collective-permute-start.2
  14.5 0.1 collective-permute-start.1
  14.6 1.9 %collective-permute-start.7 = (f32[512,128]{1,0:T(8,128)S(1)}, f32[512,128]{1,0:T(8,128)S(1)}, u32[]{:S(2)}, u32[]{:S(2)}) collective-permute-start(f32[512,128]{1,0:T(8,128)S(1)} %get-tuple-element.83), channel_id=1, source_target_pairs={{0,1},{1,0},{2,3},{3,2},{4,5},{5,4},{6,7},{7,6},{8,9},{9,8},{10,11... | collective-permute-start | bytes 786440 | tf_op jit(solution)/shard_map/ppermute | solution.py:285
  16.5 0.0 collective-permute-done.3.other_ref
  16.5 0.2 expand_weights.1.last_ref
  16.7 0.0 collective-permute-done.2.other_ref
  16.7 0.2 expand.8
  16.9 1.6 %collective-permute-start.5 = (f32[512,128]{1,0:T(8,128)S(1)}, f32[512,128]{1,0:T(8,128)S(1)}, u32[]{:S(2)}, u32[]{:S(2)}) collective-permute-start(f32[512,128]{1,0:T(8,128)S(1)} %expand.8), channel_id=1, source_target_pairs={{0,4},{2,6},{4,0},{6,2},{8,12},{10,14},{12,8},{14,10},{16,20},{18,... | collective-permute-start | bytes 786440 | tf_op jit(solution)/shard_map/ppermute | solution.py:285
  18.5 2.9 %collective-permute-done.4.refs_1_ = f32[512,128]{1,0:T(8,128)S(1)} collective-permute-done((f32[512,128]{1,0:T(8,128)S(1)}, f32[512,128]{1,0:T(8,128)S(1)}, u32[]{:S(2)}, u32[]{:S(2)}) %collective-permute-start.4) | collective-permute-done | bytes 262176 | tf_op jit(solution)/shard_map/ppermute | solution.py:285
  21.4 1.2 %row_side.5 = (f32[256,128]{1,0:T(8,128)S(1)}, f32[256,128]{1,0:T(8,128)S(1)}, f32[256,128]{1,0:T(8,128)S(1)}, f32[256,128]{1,0:T(8,128)S(1)}) custom-call(f32[512,128]{1,0:T(8,128)S(1)} %get-tuple-element.73.refs_0_, f32[512,128]{1,0:T(8,128)S(1)} %collective-permute-done.4.refs_1_, bf16[4,8,128,256]{3,2,1,0:T(8,128)(2,1)S(1)} %get-tuple-element.66.refs_2_), custom_call_target="tpu_custom_call" | custom-call | flops 20000000000 | bytes 100000 | tf_op jit(solution)/shard_map/row_side/pallas_call | solution.py:262
  22.6 0.0 collective-permute-done.1.other_ref
  22.6 0.1 collective-permute-start.6
  22.7 0.5 collective-permute-start.10
  23.2 0.0 collective-permute-start.11
  23.2 0.2 expand.9
  23.5 0.6 %collective-permute-done.6.other_ref = f32[256,128]{1,0:T(8,128)S(1)} collective-permute-done((f32[256,128]{1,0:T(8,128)S(1)}, f32[256,128]{1,0:T(8,128)S(1)}, u32[]{:S(2)}, u32[]{:S(2)}) %collective-permute-start.6) | collective-permute-done | bytes 131104 | tf_op jit(solution)/shard_map/ppermute | solution.py:285
  24.1 0.2 expand.10
  24.3 1.6 %collective-permute-start.14 = (f32[512,128]{1,0:T(8,128)S(1)}, f32[512,128]{1,0:T(8,128)S(1)}, u32[]{:S(2)}, u32[]{:S(2)}) collective-permute-start(f32[512,128]{1,0:T(8,128)S(1)} %expand.10), channel_id=1, source_target_pairs={{0,4},{2,6},{4,0},{6,2},{8,12},{10,14},{12,8},{14,10},{16,20},{18,... | collective-permute-start | bytes 786440 | tf_op jit(solution)/shard_map/ppermute | solution.py:285
  25.9 0.0 collective-permute-done.7.refs_1_
  25.9 1.2 %row_side.6 = (f32[256,128]{1,0:T(8,128)S(1)}, f32[256,128]{1,0:T(8,128)S(1)}, f32[256,128]{1,0:T(8,128)S(1)}, f32[256,128]{1,0:T(8,128)S(1)}) custom-call(f32[512,128]{1,0:T(8,128)S(1)} %get-tuple-element.81.refs_0_, f32[512,128]{1,0:T(8,128)S(1)} %collective-permute-done.7.refs_1_, bf16[4,8,128,256]{3,2,1,0:T(8,128)(2,1)S(1)} %get-tuple-element.66.refs_2_), custom_call_target="tpu_custom_call" | custom-call | flops 20000000000 | bytes 100000 | tf_op jit(solution)/shard_map/row_side/pallas_call | solution.py:262
  27.1 0.1 collective-permute-start.9
  27.2 0.0 collective-permute-done.10.other_ref
  27.2 0.5 collective-permute-start.13
  27.7 0.2 expand.11
  27.9 1.6 %collective-permute-start.8 = (f32[256,128]{1,0:T(8,128)S(1)}, f32[256,128]{1,0:T(8,128)S(1)}, u32[]{:S(2)}, u32[]{:S(2)}) collective-permute-start(f32[256,128]{1,0:T(8,128)S(1)} %slice_add_fusion.3), channel_id=1, source_target_pairs={{0,8},{2,10},{4,12},{6,14},{8,0},{10,2},{12,4},{14,6},{16,24},{18,... | collective-permute-start | bytes 393224 | tf_op jit(solution)/shard_map/ppermute | solution.py:285
  29.6 0.0 collective-permute-done.9.other_ref
  29.6 0.2 expand.12
  29.8 1.3 %collective-permute-start.19 = (f32[512,128]{1,0:T(8,128)S(1)}, f32[512,128]{1,0:T(8,128)S(1)}, u32[]{:S(2)}, u32[]{:S(2)}) collective-permute-start(f32[512,128]{1,0:T(8,128)S(1)} %expand.12), channel_id=1, source_target_pairs={{0,4},{2,6},{4,0},{6,2},{8,12},{10,14},{12,8},{14,10},{16,20},{18,... | collective-permute-start | bytes 786440 | tf_op jit(solution)/shard_map/ppermute | solution.py:285
  31.1 0.4 collective-permute-done.11.refs_1_
  31.5 1.2 %row_side.7 = (f32[256,128]{1,0:T(8,128)S(1)}, f32[256,128]{1,0:T(8,128)S(1)}, f32[256,128]{1,0:T(8,128)S(1)}, f32[256,128]{1,0:T(8,128)S(1)}) custom-call(f32[512,128]{1,0:T(8,128)S(1)} %get-tuple-element.92.refs_0_, f32[512,128]{1,0:T(8,128)S(1)} %collective-permute-done.11.refs_1_, bf16[4,8,128,256]{3,2,1,0:T(8,128)(2,1)S(1)} %get-tuple-element.66.refs_2_), custom_call_target="tpu_custom_call" | custom-call | flops 20000000000 | bytes 100000 | tf_op jit(solution)/shard_map/row_side/pallas_call | solution.py:262
  32.7 0.1 collective-permute-start.12
  32.8 0.5 collective-permute-start.16
  33.3 0.2 expand.13
  33.5 0.0 collective-permute-done.14
  33.6 1.6 %collective-permute-start.18 = (f32[256,128]{1,0:T(8,128)S(1)}, f32[256,128]{1,0:T(8,128)S(1)}, u32[]{:S(2)}, u32[]{:S(2)}) collective-permute-start(f32[256,128]{1,0:T(8,128)S(1)} %slice_add_fusion.2), channel_id=1, source_target_pairs={{0,8},{2,10},{4,12},{6,14},{8,0},{10,2},{12,4},{14,6},{16,24},{18,... | collective-permute-start | bytes 393224 | tf_op jit(solution)/shard_map/ppermute | solution.py:285
  35.2 0.2 expand.14
  35.4 1.6 %collective-permute-start.17 = (f32[512,128]{1,0:T(8,128)S(1)}, f32[512,128]{1,0:T(8,128)S(1)}, u32[]{:S(2)}, u32[]{:S(2)}) collective-permute-start(f32[512,128]{1,0:T(8,128)S(1)} %expand.14), channel_id=1, source_target_pairs={{0,4},{2,6},{4,0},{6,2},{8,12},{10,14},{12,8},{14,10},{16,20},{18,... | collective-permute-start | bytes 786440 | tf_op jit(solution)/shard_map/ppermute | solution.py:285
  37.0 0.0 collective-permute-done.8
  37.1 0.0 collective-permute-done.16.other_ref
  37.1 2.7 %collective-permute-start.15 = (f32[128,128]{1,0:T(8,128)S(1)}, f32[128,128]{1,0:T(8,128)S(1)}, u32[]{:S(2)}, u32[]{:S(2)}) collective-permute-start(f32[128,128]{1,0:T(8,128)S(1)} %fusion.9), channel_id=1, source_target_pairs={{0,16},{2,18},{4,20},{6,22},{8,24},{10,26},{12,28},{14,30},{16,0},... | collective-permute-start | bytes 196616 | tf_op jit(solution)/shard_map/ppermute | solution.py:285
  39.7 0.2 expand.15
  40.0 0.8 %collective-permute-start.21 = (f32[256,128]{1,0:T(8,128)S(1)}, f32[256,128]{1,0:T(8,128)S(1)}, u32[]{:S(2)}, u32[]{:S(2)}) collective-permute-start(f32[256,128]{1,0:T(8,128)S(1)} %slice_add_fusion.1), channel_id=1, source_target_pairs={{0,8},{2,10},{4,12},{6,14},{8,0},{10,2},{12,4},{14,6},{16,24},{18,... | collective-permute-start | bytes 393224 | tf_op jit(solution)/shard_map/ppermute | solution.py:285
  40.8 0.0 collective-permute-done.18
  40.8 2.7 %collective-permute-start.22 = (f32[128,128]{1,0:T(8,128)S(1)}, f32[128,128]{1,0:T(8,128)S(1)}, u32[]{:S(2)}, u32[]{:S(2)}) collective-permute-start(f32[128,128]{1,0:T(8,128)S(1)} %fusion.7), channel_id=1, source_target_pairs={{0,16},{2,18},{4,20},{6,22},{8,24},{10,26},{12,28},{14,30},{16,0},... | collective-permute-start | bytes 196616 | tf_op jit(solution)/shard_map/ppermute | solution.py:285
  43.5 0.5 collective-permute-done.17
  44.0 1.6 %collective-permute-start.20 = (f32[256,128]{1,0:T(8,128)S(1)}, f32[256,128]{1,0:T(8,128)S(1)}, u32[]{:S(2)}, u32[]{:S(2)}) collective-permute-start(f32[256,128]{1,0:T(8,128)S(1)} %slice_add_fusion), channel_id=1, source_target_pairs={{0,8},{2,10},{4,12},{6,14},{8,0},{10,2},{12,4},{14,6},{16,24},{18,... | collective-permute-start | bytes 393224 | tf_op jit(solution)/shard_map/ppermute | solution.py:285
  45.6 1.4 %collective-permute-done.21 = f32[256,128]{1,0:T(8,128)S(1)} collective-permute-done((f32[256,128]{1,0:T(8,128)S(1)}, f32[256,128]{1,0:T(8,128)S(1)}, u32[]{:S(2)}, u32[]{:S(2)}) %collective-permute-start.21) | collective-permute-done | bytes 131104 | tf_op jit(solution)/shard_map/ppermute | solution.py:285
  47.1 1.2 %collective-permute-start.23 = (f32[128,128]{1,0:T(8,128)S(1)}, f32[128,128]{1,0:T(8,128)S(1)}, u32[]{:S(2)}, u32[]{:S(2)}) collective-permute-start(f32[128,128]{1,0:T(8,128)S(1)} %fusion.6), channel_id=1, source_target_pairs={{0,16},{2,18},{4,20},{6,22},{8,24},{10,26},{12,28},{14,30},{16,0},... | collective-permute-start | bytes 196616 | tf_op jit(solution)/shard_map/ppermute | solution.py:285
  48.3 1.8 %collective-permute-done.20 = f32[256,128]{1,0:T(8,128)S(1)} collective-permute-done((f32[256,128]{1,0:T(8,128)S(1)}, f32[256,128]{1,0:T(8,128)S(1)}, u32[]{:S(2)}, u32[]{:S(2)}) %collective-permute-start.20) | collective-permute-done | bytes 131104 | tf_op jit(solution)/shard_map/ppermute | solution.py:285
  50.2 2.0 %collective-permute-start.24 = (f32[128,128]{1,0:T(8,128)S(1)}, f32[128,128]{1,0:T(8,128)S(1)}, u32[]{:S(2)}, u32[]{:S(2)}) collective-permute-start(f32[128,128]{1,0:T(8,128)S(1)} %fusion.8), channel_id=1, source_target_pairs={{0,16},{2,18},{4,20},{6,22},{8,24},{10,26},{12,28},{14,30},{16,0},... | collective-permute-start | bytes 196616 | tf_op jit(solution)/shard_map/ppermute | solution.py:285
  52.2 0.0 collective-permute-done.15
  52.2 2.1 %collective-permute-done.23 = f32[128,128]{1,0:T(8,128)S(1)} collective-permute-done((f32[128,128]{1,0:T(8,128)S(1)}, f32[128,128]{1,0:T(8,128)S(1)}, u32[]{:S(2)}, u32[]{:S(2)}) %collective-permute-start.23) | collective-permute-done | bytes 65568 | tf_op jit(solution)/shard_map/ppermute | solution.py:285
  54.3 1.8 %collective-permute-done.24 = f32[128,128]{1,0:T(8,128)S(1)} collective-permute-done((f32[128,128]{1,0:T(8,128)S(1)}, f32[128,128]{1,0:T(8,128)S(1)}, u32[]{:S(2)}, u32[]{:S(2)}) %collective-permute-start.24) | collective-permute-done | bytes 65568 | tf_op jit(solution)/shard_map/ppermute | solution.py:285
  56.1 0.7 %pad_maximum_fusion = f32[128,512]{1,0:T(8,128)} fusion(f32[128,128]{1,0:T(8,128)S(1)} %fusion.1, f32[128,128]{1,0:T(8,128)S(1)} %fusion.3, f32[128,128]{1,0:T(8,128)S(1)} %fusion.5, f32[128,128]{1,0:T(8,128)S(1)} %fusion.11), kind=kLoop, calls=%fused_computation | loop fusion | flops 196608 | bytes 524288 | tf_op jit(solution)/shard_map/concatenate | solution.py:350
  (19 shorter events, 0.2 us)
Async XLA Ops:
  3.5 8.9 %copy-start = (f32[1,16,128,64]{2,3,1,0:T(8,128)S(1)}, f32[1,16,128,64]{2,3,1,0:T(8,128)}, u32[]{:S(2)}) copy-start(f32[1,16,128,64]{2,3,1,0:T(8,128)} %param.11) | copy-start | bytes 1572868
  3.5 8.9 %copy-start.1 = (f32[1,4,8,128,128]{4,3,2,1,0:T(8,128)S(1)}, f32[1,4,8,128,128]{4,3,2,1,0:T(8,128)}, u32[]{:S(2)}) copy-start(f32[1,4,8,128,128]{4,3,2,1,0:T(8,128)} %param.10) | copy-start | bytes 6291460
  3.5 9.3 %collective-permute-start = (f32[512,128]{1,0:T(8,128)S(1)}, f32[512,128]{1,0:T(8,128)S(1)}, u32[]{:S(2)}, u32[]{:S(2)}) collective-permute-start(f32[512,128]{1,0:T(8,128)S(1)} %get-tuple-element.61), channel_id=1, source_target_pairs={{0,1},{1,0},{2,3},{3,2},{4,5},{5,4},{6,7},{7,6},{8,9},{9,8},{10,11... | collective-permute-start | bytes 786440 | tf_op jit(solution)/shard_map/ppermute | solution.py:285
  12.1 9.3 %collective-permute-start.4 = (f32[512,128]{1,0:T(8,128)S(1)}, f32[512,128]{1,0:T(8,128)S(1)}, u32[]{:S(2)}, u32[]{:S(2)}) collective-permute-start(f32[512,128]{1,0:T(8,128)S(1)} %get-tuple-element.74), channel_id=1, source_target_pairs={{0,1},{1,0},{2,3},{3,2},{4,5},{5,4},{6,7},{7,6},{8,9},{9,8},{10,11... | collective-permute-start | bytes 786440 | tf_op jit(solution)/shard_map/ppermute | solution.py:285
  12.7 3.8 %collective-permute-start.3 = (f32[16,64,128]{2,1,0:T(8,128)S(1)}, f32[16,64,128]{2,1,0:T(8,128)S(1)}, u32[]{:S(2)}, u32[]{:S(2)}) collective-permute-start(f32[16,64,128]{2,1,0:T(8,128)S(1)} %get-tuple-element.72), channel_id=1, source_target_pairs={{0,2},{2,0},{4,6},{6,4},{8,10},{10,8},{12,14},{14,12},{16,18},{18,... | collective-permute-start | bytes 1572872 | tf_op jit(solution)/shard_map/ppermute | solution.py:285
  14.0 2.7 %collective-permute-start.2 = (f32[256,128]{1,0:T(8,128)S(1)}, f32[256,128]{1,0:T(8,128)S(1)}, u32[]{:S(2)}, u32[]{:S(2)}) collective-permute-start(f32[256,128]{1,0:T(8,128)S(1)} %get-tuple-element.71), channel_id=1, source_target_pairs={{0,2},{2,0},{4,6},{6,4},{8,10},{10,8},{12,14},{14,12},{16,18},{18,... | collective-permute-start | bytes 393224 | tf_op jit(solution)/shard_map/ppermute | solution.py:285
  14.5 8.1 %collective-permute-start.1 = (f32[256,128]{1,0:T(8,128)S(1)}, f32[256,128]{1,0:T(8,128)S(1)}, u32[]{:S(2)}, u32[]{:S(2)}) collective-permute-start(f32[256,128]{1,0:T(8,128)S(1)} %get-tuple-element.68), channel_id=1, source_target_pairs={{0,2},{2,0},{4,6},{6,4},{8,10},{10,8},{12,14},{14,12},{16,18},{18,... | collective-permute-start | bytes 393224 | tf_op jit(solution)/shard_map/ppermute | solution.py:285
  14.6 11.3 %collective-permute-start.7 = (f32[512,128]{1,0:T(8,128)S(1)}, f32[512,128]{1,0:T(8,128)S(1)}, u32[]{:S(2)}, u32[]{:S(2)}) collective-permute-start(f32[512,128]{1,0:T(8,128)S(1)} %get-tuple-element.83), channel_id=1, source_target_pairs={{0,1},{1,0},{2,3},{3,2},{4,5},{5,4},{6,7},{7,6},{8,9},{9,8},{10,11... | collective-permute-start | bytes 786440 | tf_op jit(solution)/shard_map/ppermute | solution.py:285
  16.9 11.0 %collective-permute-start.5 = (f32[512,128]{1,0:T(8,128)S(1)}, f32[512,128]{1,0:T(8,128)S(1)}, u32[]{:S(2)}, u32[]{:S(2)}) collective-permute-start(f32[512,128]{1,0:T(8,128)S(1)} %expand.8), channel_id=1, source_target_pairs={{0,4},{2,6},{4,0},{6,2},{8,12},{10,14},{12,8},{14,10},{16,20},{18,... | collective-permute-start | bytes 786440 | tf_op jit(solution)/shard_map/ppermute | solution.py:285
  22.6 1.4 %collective-permute-start.6 = (f32[256,128]{1,0:T(8,128)S(1)}, f32[256,128]{1,0:T(8,128)S(1)}, u32[]{:S(2)}, u32[]{:S(2)}) collective-permute-start(f32[256,128]{1,0:T(8,128)S(1)} %get-tuple-element.79), channel_id=1, source_target_pairs={{0,2},{2,0},{4,6},{6,4},{8,10},{10,8},{12,14},{14,12},{16,18},{18,... | collective-permute-start | bytes 393224 | tf_op jit(solution)/shard_map/ppermute | solution.py:285
  22.7 4.4 %collective-permute-start.10 = (f32[256,128]{1,0:T(8,128)S(1)}, f32[256,128]{1,0:T(8,128)S(1)}, u32[]{:S(2)}, u32[]{:S(2)}) collective-permute-start(f32[256,128]{1,0:T(8,128)S(1)} %get-tuple-element.89), channel_id=1, source_target_pairs={{0,2},{2,0},{4,6},{6,4},{8,10},{10,8},{12,14},{14,12},{16,18},{18,... | collective-permute-start | bytes 393224 | tf_op jit(solution)/shard_map/ppermute | solution.py:285
  23.2 8.3 %collective-permute-start.11 = (f32[512,128]{1,0:T(8,128)S(1)}, f32[512,128]{1,0:T(8,128)S(1)}, u32[]{:S(2)}, u32[]{:S(2)}) collective-permute-start(f32[512,128]{1,0:T(8,128)S(1)} %get-tuple-element.94), channel_id=1, source_target_pairs={{0,1},{1,0},{2,3},{3,2},{4,5},{5,4},{6,7},{7,6},{8,9},{9,8},{10,11... | collective-permute-start | bytes 786440 | tf_op jit(solution)/shard_map/ppermute | solution.py:285
  24.3 9.2 %collective-permute-start.14 = (f32[512,128]{1,0:T(8,128)S(1)}, f32[512,128]{1,0:T(8,128)S(1)}, u32[]{:S(2)}, u32[]{:S(2)}) collective-permute-start(f32[512,128]{1,0:T(8,128)S(1)} %expand.10), channel_id=1, source_target_pairs={{0,4},{2,6},{4,0},{6,2},{8,12},{10,14},{12,8},{14,10},{16,20},{18,... | collective-permute-start | bytes 786440 | tf_op jit(solution)/shard_map/ppermute | solution.py:285
  27.1 2.5 %collective-permute-start.9 = (f32[256,128]{1,0:T(8,128)S(1)}, f32[256,128]{1,0:T(8,128)S(1)}, u32[]{:S(2)}, u32[]{:S(2)}) collective-permute-start(f32[256,128]{1,0:T(8,128)S(1)} %get-tuple-element.87), channel_id=1, source_target_pairs={{0,2},{2,0},{4,6},{6,4},{8,10},{10,8},{12,14},{14,12},{16,18},{18,... | collective-permute-start | bytes 393224 | tf_op jit(solution)/shard_map/ppermute | solution.py:285
  27.2 5.5 %collective-permute-start.13 = (f32[256,128]{1,0:T(8,128)S(1)}, f32[256,128]{1,0:T(8,128)S(1)}, u32[]{:S(2)}, u32[]{:S(2)}) collective-permute-start(f32[256,128]{1,0:T(8,128)S(1)} %get-tuple-element.99), channel_id=1, source_target_pairs={{0,2},{2,0},{4,6},{6,4},{8,10},{10,8},{12,14},{14,12},{16,18},{18,... | collective-permute-start | bytes 393224 | tf_op jit(solution)/shard_map/ppermute | solution.py:285
  27.9 9.1 %collective-permute-start.8 = (f32[256,128]{1,0:T(8,128)S(1)}, f32[256,128]{1,0:T(8,128)S(1)}, u32[]{:S(2)}, u32[]{:S(2)}) collective-permute-start(f32[256,128]{1,0:T(8,128)S(1)} %slice_add_fusion.3), channel_id=1, source_target_pairs={{0,8},{2,10},{4,12},{6,14},{8,0},{10,2},{12,4},{14,6},{16,24},{18,... | collective-permute-start | bytes 393224 | tf_op jit(solution)/shard_map/ppermute | solution.py:285
  29.8 10.1 %collective-permute-start.19 = (f32[512,128]{1,0:T(8,128)S(1)}, f32[512,128]{1,0:T(8,128)S(1)}, u32[]{:S(2)}, u32[]{:S(2)}) collective-permute-start(f32[512,128]{1,0:T(8,128)S(1)} %expand.12), channel_id=1, source_target_pairs={{0,4},{2,6},{4,0},{6,2},{8,12},{10,14},{12,8},{14,10},{16,20},{18,... | collective-permute-start | bytes 786440 | tf_op jit(solution)/shard_map/ppermute | solution.py:285
  32.7 2.5 %collective-permute-start.12 = (f32[256,128]{1,0:T(8,128)S(1)}, f32[256,128]{1,0:T(8,128)S(1)}, u32[]{:S(2)}, u32[]{:S(2)}) collective-permute-start(f32[256,128]{1,0:T(8,128)S(1)} %get-tuple-element.97), channel_id=1, source_target_pairs={{0,2},{2,0},{4,6},{6,4},{8,10},{10,8},{12,14},{14,12},{16,18},{18,... | collective-permute-start | bytes 393224 | tf_op jit(solution)/shard_map/ppermute | solution.py:285
  32.8 4.3 %collective-permute-start.16 = (f32[256,128]{1,0:T(8,128)S(1)}, f32[256,128]{1,0:T(8,128)S(1)}, u32[]{:S(2)}, u32[]{:S(2)}) collective-permute-start(f32[256,128]{1,0:T(8,128)S(1)} %get-tuple-element.105), channel_id=1, source_target_pairs={{0,2},{2,0},{4,6},{6,4},{8,10},{10,8},{12,14},{14,12},{16,18},{18,... | collective-permute-start | bytes 393224 | tf_op jit(solution)/shard_map/ppermute | solution.py:285
  33.6 7.2 %collective-permute-start.18 = (f32[256,128]{1,0:T(8,128)S(1)}, f32[256,128]{1,0:T(8,128)S(1)}, u32[]{:S(2)}, u32[]{:S(2)}) collective-permute-start(f32[256,128]{1,0:T(8,128)S(1)} %slice_add_fusion.2), channel_id=1, source_target_pairs={{0,8},{2,10},{4,12},{6,14},{8,0},{10,2},{12,4},{14,6},{16,24},{18,... | collective-permute-start | bytes 393224 | tf_op jit(solution)/shard_map/ppermute | solution.py:285
  35.4 8.5 %collective-permute-start.17 = (f32[512,128]{1,0:T(8,128)S(1)}, f32[512,128]{1,0:T(8,128)S(1)}, u32[]{:S(2)}, u32[]{:S(2)}) collective-permute-start(f32[512,128]{1,0:T(8,128)S(1)} %expand.14), channel_id=1, source_target_pairs={{0,4},{2,6},{4,0},{6,2},{8,12},{10,14},{12,8},{14,10},{16,20},{18,... | collective-permute-start | bytes 786440 | tf_op jit(solution)/shard_map/ppermute | solution.py:285
  37.1 15.1 %collective-permute-start.15 = (f32[128,128]{1,0:T(8,128)S(1)}, f32[128,128]{1,0:T(8,128)S(1)}, u32[]{:S(2)}, u32[]{:S(2)}) collective-permute-start(f32[128,128]{1,0:T(8,128)S(1)} %fusion.9), channel_id=1, source_target_pairs={{0,16},{2,18},{4,20},{6,22},{8,24},{10,26},{12,28},{14,30},{16,0},... | collective-permute-start | bytes 196616 | tf_op jit(solution)/shard_map/ppermute | solution.py:285
  40.0 7.1 %collective-permute-start.21 = (f32[256,128]{1,0:T(8,128)S(1)}, f32[256,128]{1,0:T(8,128)S(1)}, u32[]{:S(2)}, u32[]{:S(2)}) collective-permute-start(f32[256,128]{1,0:T(8,128)S(1)} %slice_add_fusion.1), channel_id=1, source_target_pairs={{0,8},{2,10},{4,12},{6,14},{8,0},{10,2},{12,4},{14,6},{16,24},{18,... | collective-permute-start | bytes 393224 | tf_op jit(solution)/shard_map/ppermute | solution.py:285
  40.8 11.4 %collective-permute-start.22 = (f32[128,128]{1,0:T(8,128)S(1)}, f32[128,128]{1,0:T(8,128)S(1)}, u32[]{:S(2)}, u32[]{:S(2)}) collective-permute-start(f32[128,128]{1,0:T(8,128)S(1)} %fusion.7), channel_id=1, source_target_pairs={{0,16},{2,18},{4,20},{6,22},{8,24},{10,26},{12,28},{14,30},{16,0},... | collective-permute-start | bytes 196616 | tf_op jit(solution)/shard_map/ppermute | solution.py:285
  44.0 6.2 %collective-permute-start.20 = (f32[256,128]{1,0:T(8,128)S(1)}, f32[256,128]{1,0:T(8,128)S(1)}, u32[]{:S(2)}, u32[]{:S(2)}) collective-permute-start(f32[256,128]{1,0:T(8,128)S(1)} %slice_add_fusion), channel_id=1, source_target_pairs={{0,8},{2,10},{4,12},{6,14},{8,0},{10,2},{12,4},{14,6},{16,24},{18,... | collective-permute-start | bytes 393224 | tf_op jit(solution)/shard_map/ppermute | solution.py:285
  47.1 7.2 %collective-permute-start.23 = (f32[128,128]{1,0:T(8,128)S(1)}, f32[128,128]{1,0:T(8,128)S(1)}, u32[]{:S(2)}, u32[]{:S(2)}) collective-permute-start(f32[128,128]{1,0:T(8,128)S(1)} %fusion.6), channel_id=1, source_target_pairs={{0,16},{2,18},{4,20},{6,22},{8,24},{10,26},{12,28},{14,30},{16,0},... | collective-permute-start | bytes 196616 | tf_op jit(solution)/shard_map/ppermute | solution.py:285
  50.2 5.9 %collective-permute-start.24 = (f32[128,128]{1,0:T(8,128)S(1)}, f32[128,128]{1,0:T(8,128)S(1)}, u32[]{:S(2)}, u32[]{:S(2)}) collective-permute-start(f32[128,128]{1,0:T(8,128)S(1)} %fusion.8), channel_id=1, source_target_pairs={{0,16},{2,18},{4,20},{6,22},{8,24},{10,26},{12,28},{14,30},{16,0},... | collective-permute-start | bytes 196616 | tf_op jit(solution)/shard_map/ppermute | solution.py:285

commit v4 on v3

--- a/solution.py
+++ b/solution.py
@@ -327,7 +327,7 @@
         done = []
         if c >= 1:
             done.append(low_half(c - 1, own_high))
-        if c >= 2:
+        if 2 <= c < last:
             done.append(forward([c - 2], 2, own_high))
         got = swap(high, "tile", n_tile, 1)
         if done:
@@ -338,7 +338,7 @@
             received[c + 2] = exchange(parts[c + 2], own_high)
     low_half(last, sends[last, 1])
     done = [sends[last, 1]]
-    for c, b in ((last - 3, 3), (last - 1, 2), (last - 2, 3), (last, 2), (last - 1, 3), (last, 3)):
+    for c, b in ((last - 2, 2), (last - 3, 3), (last - 1, 2), (last - 2, 3), (last, 2), (last - 1, 3), (last, 3)):
         if b < bits and (c, b) not in sends:
             done = [forward([c], b, *done)]
     done = done[0]

time: 57 us -> 57.7 us (1.012)
  starting transfers between devices: 27.8 us -> 28.8 us
    ppermute x25, starting transfers between devices: 27.8 us -> 28.8 us  [swap(): return lax.ppermute(x, axis, [(i, i ^ mask) for i in range(size)])]
where the time goes in v4:
time: 57.7 us; the launch traced here: 57.6 us
  starting transfers between devices  28.8 us (50%)
  Pallas kernels  16.2 us (28%)
  waiting for transfers between devices  11.3 us (20%)
  other arithmetic  0.9 us (2%)
    ppermute x25, starting transfers between devices, swap(): return lax.ppermute(x, axis, [(i, i ^ mask) for i in range(size)])  28.8 us
    ppermute x25, waiting for transfers between devices, swap(): return lax.ppermute(x, axis, [(i, i ^ mask) for i in range(size)])  11.3 us
    pallas_call x2, Pallas kernels, column_side(): pl.pallas_call(functools.partial(column_kernel, n_seg, pieces, start * CH...  9.1 us
    pallas_call x4, Pallas kernels, row_side(): pl.pallas_call(functools.partial(row_kernel, n_seg, n_tile, leaf), in_spe...  4.72 us
    pallas_call x8, Pallas kernels, expanded(): pl.pallas_call(functools.partial(expand_kernel, part), in_specs=[in_vmem]...  1.89 us
  transfers between devices with their start and end apart: 25, of which 8 were waited for; matrix products, arithmetic and copies ran while one was open for 0% of the time, Pallas kernels for 22%

profile of v4, /device:TPU:0, one launch (start us, length us, event | category | flops | bytes accessed | tf_op | source)
XLA Modules:
  0.0 57.6 jit_solution(16405058162375773814)
XLA Ops:
  0.0 3.4 %column_side.2 = (f32[512,128]{1,0:T(8,128)S(1)}, f32[512,128]{1,0:T(8,128)S(1)}) custom-call(f32[2048,512]{1,0:T(8,128)} %x_hbm.3, f32[16,64,128]{2,1,0:T(8,128)} %bitcast.12, f32[4,8,128,128]{3,2,1,0:T(8,128)} %bitcast.10, f32[16,64,64]{2,1,0:T(8,128)} %bitcast.14), custom_call_target="tpu_custom_call" | custom-call | flops 1000000 | bytes 100000 | tf_op jit(solution)/shard_map/column_side/pallas_call | solution.py:216
  3.5 0.0 copy-start
  3.5 0.0 copy-start.1
  3.5 3.0 %collective-permute-start = (f32[512,128]{1,0:T(8,128)S(1)}, f32[512,128]{1,0:T(8,128)S(1)}, u32[]{:S(2)}, u32[]{:S(2)}) collective-permute-start(f32[512,128]{1,0:T(8,128)S(1)} %get-tuple-element.61), channel_id=1, source_target_pairs={{0,1},{1,0},{2,3},{3,2},{4,5},{5,4},{6,7},{7,6},{8,9},{9,8},{10,11... | collective-permute-start | bytes 786440 | tf_op jit(solution)/shard_map/ppermute | solution.py:285
  6.5 5.7 %column_side.3 = (f32[512,128]{1,0:T(8,128)S(1)}, f32[512,128]{1,0:T(8,128)S(1)}, f32[512,128]{1,0:T(8,128)S(1)}, f32[512,128]{1,0:T(8,128)S(1)}, f32[512,128]{1,0:T(8,128)S(1)}, /*index=5*/f32[512,128]{1,0:T(8,128)S(1)}) custom-call(f32[2048,512]{1,0:T(8,128)} %x_hbm.3, f32[16,64,128]{2,1,0:T(8,128)} %bitcast.13, f32[4,8,128,128]{3,2,1,0:T(8,128)} %bitcast.11, ...), custom_call_target="tpu_custom_call" | custom-call | flops 1000000 | bytes 100000 | tf_op jit(solution)/shard_map/column_side/pallas_call | solution.py:216
  12.1 0.2 collective-permute-start.4
  12.4 0.3 row_weights.1
  12.7 0.1 collective-permute-start.3
  12.8 0.0 collective-permute-done.refs_1_
  12.8 1.2 %row_side.4 = (f32[256,128]{1,0:T(8,128)S(1)}, f32[256,128]{1,0:T(8,128)S(1)}, f32[256,128]{1,0:T(8,128)S(1)}, f32[256,128]{1,0:T(8,128)S(1)}) custom-call(f32[512,128]{1,0:T(8,128)S(1)} %get-tuple-element.64.refs_0_, f32[512,128]{1,0:T(8,128)S(1)} %collective-permute-done.refs_1_, bf16[4,8,128,256]{3,2,1,0:T(8,128)(2,1)S(1)} %get-tuple-element.66.refs_2_), custom_call_target="tpu_custom_call" | custom-call | flops 20000000000 | bytes 100000 | tf_op jit(solution)/shard_map/row_side/pallas_call | solution.py:262
  14.0 0.5 collective-permute-start.2
  14.5 0.1 collective-permute-start.1
  14.6 1.9 %collective-permute-start.7 = (f32[512,128]{1,0:T(8,128)S(1)}, f32[512,128]{1,0:T(8,128)S(1)}, u32[]{:S(2)}, u32[]{:S(2)}) collective-permute-start(f32[512,128]{1,0:T(8,128)S(1)} %get-tuple-element.83), channel_id=1, source_target_pairs={{0,1},{1,0},{2,3},{3,2},{4,5},{5,4},{6,7},{7,6},{8,9},{9,8},{10,11... | collective-permute-start | bytes 786440 | tf_op jit(solution)/shard_map/ppermute | solution.py:285
  16.5 0.2 expand_weights.1.last_ref
  16.7 0.0 collective-permute-done.2.other_ref
  16.7 0.2 expand.8
  16.9 1.6 %collective-permute-start.5 = (f32[512,128]{1,0:T(8,128)S(1)}, f32[512,128]{1,0:T(8,128)S(1)}, u32[]{:S(2)}, u32[]{:S(2)}) collective-permute-start(f32[512,128]{1,0:T(8,128)S(1)} %expand.8), channel_id=1, source_target_pairs={{0,4},{2,6},{4,0},{6,2},{8,12},{10,14},{12,8},{14,10},{16,20},{18,... | collective-permute-start | bytes 786440 | tf_op jit(solution)/shard_map/ppermute | solution.py:285
  18.5 2.9 %collective-permute-done.4.refs_1_ = f32[512,128]{1,0:T(8,128)S(1)} collective-permute-done((f32[512,128]{1,0:T(8,128)S(1)}, f32[512,128]{1,0:T(8,128)S(1)}, u32[]{:S(2)}, u32[]{:S(2)}) %collective-permute-start.4) | collective-permute-done | bytes 262176 | tf_op jit(solution)/shard_map/ppermute | solution.py:285
  21.4 1.2 %row_side.5 = (f32[256,128]{1,0:T(8,128)S(1)}, f32[256,128]{1,0:T(8,128)S(1)}, f32[256,128]{1,0:T(8,128)S(1)}, f32[256,128]{1,0:T(8,128)S(1)}) custom-call(f32[512,128]{1,0:T(8,128)S(1)} %get-tuple-element.73.refs_0_, f32[512,128]{1,0:T(8,128)S(1)} %collective-permute-done.4.refs_1_, bf16[4,8,128,256]{3,2,1,0:T(8,128)(2,1)S(1)} %get-tuple-element.66.refs_2_), custom_call_target="tpu_custom_call" | custom-call | flops 20000000000 | bytes 100000 | tf_op jit(solution)/shard_map/row_side/pallas_call | solution.py:262
  22.6 0.0 collective-permute-done.1.other_ref
  22.6 0.1 collective-permute-start.6
  22.7 0.5 collective-permute-start.9
  23.2 0.0 collective-permute-start.12
  23.2 0.2 expand.9
  23.5 0.6 %collective-permute-done.6.other_ref = f32[256,128]{1,0:T(8,128)S(1)} collective-permute-done((f32[256,128]{1,0:T(8,128)S(1)}, f32[256,128]{1,0:T(8,128)S(1)}, u32[]{:S(2)}, u32[]{:S(2)}) %collective-permute-start.6) | collective-permute-done | bytes 131104 | tf_op jit(solution)/shard_map/ppermute | solution.py:285
  24.1 0.2 expand.10
  24.3 1.6 %collective-permute-start.10 = (f32[512,128]{1,0:T(8,128)S(1)}, f32[512,128]{1,0:T(8,128)S(1)}, u32[]{:S(2)}, u32[]{:S(2)}) collective-permute-start(f32[512,128]{1,0:T(8,128)S(1)} %expand.10), channel_id=1, source_target_pairs={{0,4},{2,6},{4,0},{6,2},{8,12},{10,14},{12,8},{14,10},{16,20},{18,... | collective-permute-start | bytes 786440 | tf_op jit(solution)/shard_map/ppermute | solution.py:285
  25.9 0.0 collective-permute-done.7.refs_1_
  25.9 1.2 %row_side.6 = (f32[256,128]{1,0:T(8,128)S(1)}, f32[256,128]{1,0:T(8,128)S(1)}, f32[256,128]{1,0:T(8,128)S(1)}, f32[256,128]{1,0:T(8,128)S(1)}) custom-call(f32[512,128]{1,0:T(8,128)S(1)} %get-tuple-element.81.refs_0_, f32[512,128]{1,0:T(8,128)S(1)} %collective-permute-done.7.refs_1_, bf16[4,8,128,256]{3,2,1,0:T(8,128)(2,1)S(1)} %get-tuple-element.66.refs_2_), custom_call_target="tpu_custom_call" | custom-call | flops 20000000000 | bytes 100000 | tf_op jit(solution)/shard_map/row_side/pallas_call | solution.py:262
  27.1 0.1 collective-permute-start.11
  27.2 0.0 collective-permute-done.9.other_ref
  27.2 0.5 collective-permute-start.14
  27.7 0.2 expand.11
  27.9 1.6 %collective-permute-start.8 = (f32[256,128]{1,0:T(8,128)S(1)}, f32[256,128]{1,0:T(8,128)S(1)}, u32[]{:S(2)}, u32[]{:S(2)}) collective-permute-start(f32[256,128]{1,0:T(8,128)S(1)} %slice_add_fusion.3), channel_id=1, source_target_pairs={{0,8},{2,10},{4,12},{6,14},{8,0},{10,2},{12,4},{14,6},{16,24},{18,... | collective-permute-start | bytes 393224 | tf_op jit(solution)/shard_map/ppermute | solution.py:285
  29.6 0.2 expand.12
  29.8 1.3 %collective-permute-start.19 = (f32[512,128]{1,0:T(8,128)S(1)}, f32[512,128]{1,0:T(8,128)S(1)}, u32[]{:S(2)}, u32[]{:S(2)}) collective-permute-start(f32[512,128]{1,0:T(8,128)S(1)} %expand.12), channel_id=1, source_target_pairs={{0,4},{2,6},{4,0},{6,2},{8,12},{10,14},{12,8},{14,10},{16,20},{18,... | collective-permute-start | bytes 786440 | tf_op jit(solution)/shard_map/ppermute | solution.py:285
  31.1 0.4 collective-permute-done.12.refs_1_
  31.5 1.2 %row_side.7 = (f32[256,128]{1,0:T(8,128)S(1)}, f32[256,128]{1,0:T(8,128)S(1)}, f32[256,128]{1,0:T(8,128)S(1)}, f32[256,128]{1,0:T(8,128)S(1)}) custom-call(f32[512,128]{1,0:T(8,128)S(1)} %get-tuple-element.92.refs_0_, f32[512,128]{1,0:T(8,128)S(1)} %collective-permute-done.12.refs_1_, bf16[4,8,128,256]{3,2,1,0:T(8,128)(2,1)S(1)} %get-tuple-element.66.refs_2_), custom_call_target="tpu_custom_call" | custom-call | flops 20000000000 | bytes 100000 | tf_op jit(solution)/shard_map/row_side/pallas_call | solution.py:262
  32.7 0.0 collective-permute-done.14.other_ref
  32.7 0.1 collective-permute-start.13
  32.8 0.5 collective-permute-start.16
  33.3 0.2 expand.13
  33.5 0.6 %collective-permute-done.13.other_ref = f32[256,128]{1,0:T(8,128)S(1)} collective-permute-done((f32[256,128]{1,0:T(8,128)S(1)}, f32[256,128]{1,0:T(8,128)S(1)}, u32[]{:S(2)}, u32[]{:S(2)}) %collective-permute-start.13) | collective-permute-done | bytes 131104 | tf_op jit(solution)/shard_map/ppermute | solution.py:285
  34.1 0.2 expand.14
  34.4 1.6 %collective-permute-start.17 = (f32[512,128]{1,0:T(8,128)S(1)}, f32[512,128]{1,0:T(8,128)S(1)}, u32[]{:S(2)}, u32[]{:S(2)}) collective-permute-start(f32[512,128]{1,0:T(8,128)S(1)} %expand.14), channel_id=1, source_target_pairs={{0,4},{2,6},{4,0},{6,2},{8,12},{10,14},{12,8},{14,10},{16,20},{18,... | collective-permute-start | bytes 786440 | tf_op jit(solution)/shard_map/ppermute | solution.py:285
  35.9 0.0 collective-permute-done.10
  36.0 1.6 %collective-permute-start.18 = (f32[256,128]{1,0:T(8,128)S(1)}, f32[256,128]{1,0:T(8,128)S(1)}, u32[]{:S(2)}, u32[]{:S(2)}) collective-permute-start(f32[256,128]{1,0:T(8,128)S(1)} %slice_add_fusion.2), channel_id=1, source_target_pairs={{0,8},{2,10},{4,12},{6,14},{8,0},{10,2},{12,4},{14,6},{16,24},{18,... | collective-permute-start | bytes 393224 | tf_op jit(solution)/shard_map/ppermute | solution.py:285
  37.6 0.0 collective-permute-done.8
  37.6 2.7 %collective-permute-start.15 = (f32[128,128]{1,0:T(8,128)S(1)}, f32[128,128]{1,0:T(8,128)S(1)}, u32[]{:S(2)}, u32[]{:S(2)}) collective-permute-start(f32[128,128]{1,0:T(8,128)S(1)} %fusion.9), channel_id=1, source_target_pairs={{0,16},{2,18},{4,20},{6,22},{8,24},{10,26},{12,28},{14,30},{16,0},... | collective-permute-start | bytes 196616 | tf_op jit(solution)/shard_map/ppermute | solution.py:285
  40.3 0.2 expand.15
  40.5 0.0 collective-permute-done.19
  40.6 0.5 collective-permute-start.21
  41.1 0.9 %collective-permute-done.18 = f32[256,128]{1,0:T(8,128)S(1)} collective-permute-done((f32[256,128]{1,0:T(8,128)S(1)}, f32[256,128]{1,0:T(8,128)S(1)}, u32[]{:S(2)}, u32[]{:S(2)}) %collective-permute-start.18) | collective-permute-done | bytes 131104 | tf_op jit(solution)/shard_map/ppermute | solution.py:285
  42.0 3.6 %collective-permute-start.22 = (f32[128,128]{1,0:T(8,128)S(1)}, f32[128,128]{1,0:T(8,128)S(1)}, u32[]{:S(2)}, u32[]{:S(2)}) collective-permute-start(f32[128,128]{1,0:T(8,128)S(1)} %fusion.7), channel_id=1, source_target_pairs={{0,16},{2,18},{4,20},{6,22},{8,24},{10,26},{12,28},{14,30},{16,0},... | collective-permute-start | bytes 196616 | tf_op jit(solution)/shard_map/ppermute | solution.py:285
  45.6 0.0 collective-permute-done.17
  45.6 2.5 %collective-permute-start.20 = (f32[256,128]{1,0:T(8,128)S(1)}, f32[256,128]{1,0:T(8,128)S(1)}, u32[]{:S(2)}, u32[]{:S(2)}) collective-permute-start(f32[256,128]{1,0:T(8,128)S(1)} %slice_add_fusion), channel_id=1, source_target_pairs={{0,8},{2,10},{4,12},{6,14},{8,0},{10,2},{12,4},{14,6},{16,24},{18,... | collective-permute-start | bytes 393224 | tf_op jit(solution)/shard_map/ppermute | solution.py:285
  48.2 0.0 collective-permute-done.21
  48.2 0.9 %collective-permute-start.23 = (f32[128,128]{1,0:T(8,128)S(1)}, f32[128,128]{1,0:T(8,128)S(1)}, u32[]{:S(2)}, u32[]{:S(2)}) collective-permute-start(f32[128,128]{1,0:T(8,128)S(1)} %fusion.6), channel_id=1, source_target_pairs={{0,16},{2,18},{4,20},{6,22},{8,24},{10,26},{12,28},{14,30},{16,0},... | collective-permute-start | bytes 196616 | tf_op jit(solution)/shard_map/ppermute | solution.py:285
  49.0 2.5 %collective-permute-done.20 = f32[256,128]{1,0:T(8,128)S(1)} collective-permute-done((f32[256,128]{1,0:T(8,128)S(1)}, f32[256,128]{1,0:T(8,128)S(1)}, u32[]{:S(2)}, u32[]{:S(2)}) %collective-permute-start.20) | collective-permute-done | bytes 131104 | tf_op jit(solution)/shard_map/ppermute | solution.py:285
  51.6 1.9 %collective-permute-start.24 = (f32[128,128]{1,0:T(8,128)S(1)}, f32[128,128]{1,0:T(8,128)S(1)}, u32[]{:S(2)}, u32[]{:S(2)}) collective-permute-start(f32[128,128]{1,0:T(8,128)S(1)} %fusion.8), channel_id=1, source_target_pairs={{0,16},{2,18},{4,20},{6,22},{8,24},{10,26},{12,28},{14,30},{16,0},... | collective-permute-start | bytes 196616 | tf_op jit(solution)/shard_map/ppermute | solution.py:285
  53.5 0.0 collective-permute-done.22
  53.5 1.4 %collective-permute-done.23 = f32[128,128]{1,0:T(8,128)S(1)} collective-permute-done((f32[128,128]{1,0:T(8,128)S(1)}, f32[128,128]{1,0:T(8,128)S(1)}, u32[]{:S(2)}, u32[]{:S(2)}) %collective-permute-start.23) | collective-permute-done | bytes 65568 | tf_op jit(solution)/shard_map/ppermute | solution.py:285
  54.9 1.9 %collective-permute-done.24 = f32[128,128]{1,0:T(8,128)S(1)} collective-permute-done((f32[128,128]{1,0:T(8,128)S(1)}, f32[128,128]{1,0:T(8,128)S(1)}, u32[]{:S(2)}, u32[]{:S(2)}) %collective-permute-start.24) | collective-permute-done | bytes 65568 | tf_op jit(solution)/shard_map/ppermute | solution.py:285
  56.8 0.7 %pad_maximum_fusion = f32[128,512]{1,0:T(8,128)} fusion(f32[128,128]{1,0:T(8,128)S(1)} %fusion.1, f32[128,128]{1,0:T(8,128)S(1)} %fusion.3, f32[128,128]{1,0:T(8,128)S(1)} %fusion.5, f32[128,128]{1,0:T(8,128)S(1)} %fusion.11), kind=kLoop, calls=%fused_computation | loop fusion | flops 196608 | bytes 524288 | tf_op jit(solution)/shard_map/concatenate | solution.py:350
  (19 shorter events, 0.2 us)
Async XLA Ops:
  3.5 8.9 %copy-start = (f32[1,16,128,64]{2,3,1,0:T(8,128)S(1)}, f32[1,16,128,64]{2,3,1,0:T(8,128)}, u32[]{:S(2)}) copy-start(f32[1,16,128,64]{2,3,1,0:T(8,128)} %param.11) | copy-start | bytes 1572868
  3.5 8.9 %copy-start.1 = (f32[1,4,8,128,128]{4,3,2,1,0:T(8,128)S(1)}, f32[1,4,8,128,128]{4,3,2,1,0:T(8,128)}, u32[]{:S(2)}) copy-start(f32[1,4,8,128,128]{4,3,2,1,0:T(8,128)} %param.10) | copy-start | bytes 6291460
  3.5 9.3 %collective-permute-start = (f32[512,128]{1,0:T(8,128)S(1)}, f32[512,128]{1,0:T(8,128)S(1)}, u32[]{:S(2)}, u32[]{:S(2)}) collective-permute-start(f32[512,128]{1,0:T(8,128)S(1)} %get-tuple-element.61), channel_id=1, source_target_pairs={{0,1},{1,0},{2,3},{3,2},{4,5},{5,4},{6,7},{7,6},{8,9},{9,8},{10,11... | collective-permute-start | bytes 786440 | tf_op jit(solution)/shard_map/ppermute | solution.py:285
  12.1 9.3 %collective-permute-start.4 = (f32[512,128]{1,0:T(8,128)S(1)}, f32[512,128]{1,0:T(8,128)S(1)}, u32[]{:S(2)}, u32[]{:S(2)}) collective-permute-start(f32[512,128]{1,0:T(8,128)S(1)} %get-tuple-element.74), channel_id=1, source_target_pairs={{0,1},{1,0},{2,3},{3,2},{4,5},{5,4},{6,7},{7,6},{8,9},{9,8},{10,11... | collective-permute-start | bytes 786440 | tf_op jit(solution)/shard_map/ppermute | solution.py:285
  12.7 3.8 %collective-permute-start.3 = (f32[16,64,128]{2,1,0:T(8,128)S(1)}, f32[16,64,128]{2,1,0:T(8,128)S(1)}, u32[]{:S(2)}, u32[]{:S(2)}) collective-permute-start(f32[16,64,128]{2,1,0:T(8,128)S(1)} %get-tuple-element.72), channel_id=1, source_target_pairs={{0,2},{2,0},{4,6},{6,4},{8,10},{10,8},{12,14},{14,12},{16,18},{18,... | collective-permute-start | bytes 1572872 | tf_op jit(solution)/shard_map/ppermute | solution.py:285
  14.0 2.7 %collective-permute-start.2 = (f32[256,128]{1,0:T(8,128)S(1)}, f32[256,128]{1,0:T(8,128)S(1)}, u32[]{:S(2)}, u32[]{:S(2)}) collective-permute-start(f32[256,128]{1,0:T(8,128)S(1)} %get-tuple-element.71), channel_id=1, source_target_pairs={{0,2},{2,0},{4,6},{6,4},{8,10},{10,8},{12,14},{14,12},{16,18},{18,... | collective-permute-start | bytes 393224 | tf_op jit(solution)/shard_map/ppermute | solution.py:285
  14.5 8.1 %collective-permute-start.1 = (f32[256,128]{1,0:T(8,128)S(1)}, f32[256,128]{1,0:T(8,128)S(1)}, u32[]{:S(2)}, u32[]{:S(2)}) collective-permute-start(f32[256,128]{1,0:T(8,128)S(1)} %get-tuple-element.68), channel_id=1, source_target_pairs={{0,2},{2,0},{4,6},{6,4},{8,10},{10,8},{12,14},{14,12},{16,18},{18,... | collective-permute-start | bytes 393224 | tf_op jit(solution)/shard_map/ppermute | solution.py:285
  14.6 11.3 %collective-permute-start.7 = (f32[512,128]{1,0:T(8,128)S(1)}, f32[512,128]{1,0:T(8,128)S(1)}, u32[]{:S(2)}, u32[]{:S(2)}) collective-permute-start(f32[512,128]{1,0:T(8,128)S(1)} %get-tuple-element.83), channel_id=1, source_target_pairs={{0,1},{1,0},{2,3},{3,2},{4,5},{5,4},{6,7},{7,6},{8,9},{9,8},{10,11... | collective-permute-start | bytes 786440 | tf_op jit(solution)/shard_map/ppermute | solution.py:285
  16.9 11.0 %collective-permute-start.5 = (f32[512,128]{1,0:T(8,128)S(1)}, f32[512,128]{1,0:T(8,128)S(1)}, u32[]{:S(2)}, u32[]{:S(2)}) collective-permute-start(f32[512,128]{1,0:T(8,128)S(1)} %expand.8), channel_id=1, source_target_pairs={{0,4},{2,6},{4,0},{6,2},{8,12},{10,14},{12,8},{14,10},{16,20},{18,... | collective-permute-start | bytes 786440 | tf_op jit(solution)/shard_map/ppermute | solution.py:285
  22.6 1.4 %collective-permute-start.6 = (f32[256,128]{1,0:T(8,128)S(1)}, f32[256,128]{1,0:T(8,128)S(1)}, u32[]{:S(2)}, u32[]{:S(2)}) collective-permute-start(f32[256,128]{1,0:T(8,128)S(1)} %get-tuple-element.79), channel_id=1, source_target_pairs={{0,2},{2,0},{4,6},{6,4},{8,10},{10,8},{12,14},{14,12},{16,18},{18,... | collective-permute-start | bytes 393224 | tf_op jit(solution)/shard_map/ppermute | solution.py:285
  22.7 4.4 %collective-permute-start.9 = (f32[256,128]{1,0:T(8,128)S(1)}, f32[256,128]{1,0:T(8,128)S(1)}, u32[]{:S(2)}, u32[]{:S(2)}) collective-permute-start(f32[256,128]{1,0:T(8,128)S(1)} %get-tuple-element.88), channel_id=1, source_target_pairs={{0,2},{2,0},{4,6},{6,4},{8,10},{10,8},{12,14},{14,12},{16,18},{18,... | collective-permute-start | bytes 393224 | tf_op jit(solution)/shard_map/ppermute | solution.py:285
  23.2 8.3 %collective-permute-start.12 = (f32[512,128]{1,0:T(8,128)S(1)}, f32[512,128]{1,0:T(8,128)S(1)}, u32[]{:S(2)}, u32[]{:S(2)}) collective-permute-start(f32[512,128]{1,0:T(8,128)S(1)} %get-tuple-element.94), channel_id=1, source_target_pairs={{0,1},{1,0},{2,3},{3,2},{4,5},{5,4},{6,7},{7,6},{8,9},{9,8},{10,11... | collective-permute-start | bytes 786440 | tf_op jit(solution)/shard_map/ppermute | solution.py:285
  24.3 11.6 %collective-permute-start.10 = (f32[512,128]{1,0:T(8,128)S(1)}, f32[512,128]{1,0:T(8,128)S(1)}, u32[]{:S(2)}, u32[]{:S(2)}) collective-permute-start(f32[512,128]{1,0:T(8,128)S(1)} %expand.10), channel_id=1, source_target_pairs={{0,4},{2,6},{4,0},{6,2},{8,12},{10,14},{12,8},{14,10},{16,20},{18,... | collective-permute-start | bytes 786440 | tf_op jit(solution)/shard_map/ppermute | solution.py:285
  27.1 2.5 %collective-permute-start.11 = (f32[256,128]{1,0:T(8,128)S(1)}, f32[256,128]{1,0:T(8,128)S(1)}, u32[]{:S(2)}, u32[]{:S(2)}) collective-permute-start(f32[256,128]{1,0:T(8,128)S(1)} %get-tuple-element.90), channel_id=1, source_target_pairs={{0,2},{2,0},{4,6},{6,4},{8,10},{10,8},{12,14},{14,12},{16,18},{18,... | collective-permute-start | bytes 393224 | tf_op jit(solution)/shard_map/ppermute | solution.py:285
  27.2 5.5 %collective-permute-start.14 = (f32[256,128]{1,0:T(8,128)S(1)}, f32[256,128]{1,0:T(8,128)S(1)}, u32[]{:S(2)}, u32[]{:S(2)}) collective-permute-start(f32[256,128]{1,0:T(8,128)S(1)} %get-tuple-element.99), channel_id=1, source_target_pairs={{0,2},{2,0},{4,6},{6,4},{8,10},{10,8},{12,14},{14,12},{16,18},{18,... | collective-permute-start | bytes 393224 | tf_op jit(solution)/shard_map/ppermute | solution.py:285
  27.9 9.7 %collective-permute-start.8 = (f32[256,128]{1,0:T(8,128)S(1)}, f32[256,128]{1,0:T(8,128)S(1)}, u32[]{:S(2)}, u32[]{:S(2)}) collective-permute-start(f32[256,128]{1,0:T(8,128)S(1)} %slice_add_fusion.3), channel_id=1, source_target_pairs={{0,8},{2,10},{4,12},{6,14},{8,0},{10,2},{12,4},{14,6},{16,24},{18,... | collective-permute-start | bytes 393224 | tf_op jit(solution)/shard_map/ppermute | solution.py:285
  29.8 10.7 %collective-permute-start.19 = (f32[512,128]{1,0:T(8,128)S(1)}, f32[512,128]{1,0:T(8,128)S(1)}, u32[]{:S(2)}, u32[]{:S(2)}) collective-permute-start(f32[512,128]{1,0:T(8,128)S(1)} %expand.12), channel_id=1, source_target_pairs={{0,4},{2,6},{4,0},{6,2},{8,12},{10,14},{12,8},{14,10},{16,20},{18,... | collective-permute-start | bytes 786440 | tf_op jit(solution)/shard_map/ppermute | solution.py:285
  32.7 1.4 %collective-permute-start.13 = (f32[256,128]{1,0:T(8,128)S(1)}, f32[256,128]{1,0:T(8,128)S(1)}, u32[]{:S(2)}, u32[]{:S(2)}) collective-permute-start(f32[256,128]{1,0:T(8,128)S(1)} %get-tuple-element.97), channel_id=1, source_target_pairs={{0,2},{2,0},{4,6},{6,4},{8,10},{10,8},{12,14},{14,12},{16,18},{18,... | collective-permute-start | bytes 393224 | tf_op jit(solution)/shard_map/ppermute | solution.py:285
  32.8 4.9 %collective-permute-start.16 = (f32[256,128]{1,0:T(8,128)S(1)}, f32[256,128]{1,0:T(8,128)S(1)}, u32[]{:S(2)}, u32[]{:S(2)}) collective-permute-start(f32[256,128]{1,0:T(8,128)S(1)} %get-tuple-element.105), channel_id=1, source_target_pairs={{0,2},{2,0},{4,6},{6,4},{8,10},{10,8},{12,14},{14,12},{16,18},{18,... | collective-permute-start | bytes 393224 | tf_op jit(solution)/shard_map/ppermute | solution.py:285
  34.4 11.2 %collective-permute-start.17 = (f32[512,128]{1,0:T(8,128)S(1)}, f32[512,128]{1,0:T(8,128)S(1)}, u32[]{:S(2)}, u32[]{:S(2)}) collective-permute-start(f32[512,128]{1,0:T(8,128)S(1)} %expand.14), channel_id=1, source_target_pairs={{0,4},{2,6},{4,0},{6,2},{8,12},{10,14},{12,8},{14,10},{16,20},{18,... | collective-permute-start | bytes 786440 | tf_op jit(solution)/shard_map/ppermute | solution.py:285
  36.0 6.0 %collective-permute-start.18 = (f32[256,128]{1,0:T(8,128)S(1)}, f32[256,128]{1,0:T(8,128)S(1)}, u32[]{:S(2)}, u32[]{:S(2)}) collective-permute-start(f32[256,128]{1,0:T(8,128)S(1)} %slice_add_fusion.2), channel_id=1, source_target_pairs={{0,8},{2,10},{4,12},{6,14},{8,0},{10,2},{12,4},{14,6},{16,24},{18,... | collective-permute-start | bytes 393224 | tf_op jit(solution)/shard_map/ppermute | solution.py:285
  37.6 15.8 %collective-permute-start.15 = (f32[128,128]{1,0:T(8,128)S(1)}, f32[128,128]{1,0:T(8,128)S(1)}, u32[]{:S(2)}, u32[]{:S(2)}) collective-permute-start(f32[128,128]{1,0:T(8,128)S(1)} %fusion.9), channel_id=1, source_target_pairs={{0,16},{2,18},{4,20},{6,22},{8,24},{10,26},{12,28},{14,30},{16,0},... | collective-permute-start | bytes 196616 | tf_op jit(solution)/shard_map/ppermute | solution.py:285
  40.6 7.6 %collective-permute-start.21 = (f32[256,128]{1,0:T(8,128)S(1)}, f32[256,128]{1,0:T(8,128)S(1)}, u32[]{:S(2)}, u32[]{:S(2)}) collective-permute-start(f32[256,128]{1,0:T(8,128)S(1)} %slice_add_fusion.1), channel_id=1, source_target_pairs={{0,8},{2,10},{4,12},{6,14},{8,0},{10,2},{12,4},{14,6},{16,24},{18,... | collective-permute-start | bytes 393224 | tf_op jit(solution)/shard_map/ppermute | solution.py:285
  42.0 11.4 %collective-permute-start.22 = (f32[128,128]{1,0:T(8,128)S(1)}, f32[128,128]{1,0:T(8,128)S(1)}, u32[]{:S(2)}, u32[]{:S(2)}) collective-permute-start(f32[128,128]{1,0:T(8,128)S(1)} %fusion.7), channel_id=1, source_target_pairs={{0,16},{2,18},{4,20},{6,22},{8,24},{10,26},{12,28},{14,30},{16,0},... | collective-permute-start | bytes 196616 | tf_op jit(solution)/shard_map/ppermute | solution.py:285
  45.6 6.0 %collective-permute-start.20 = (f32[256,128]{1,0:T(8,128)S(1)}, f32[256,128]{1,0:T(8,128)S(1)}, u32[]{:S(2)}, u32[]{:S(2)}) collective-permute-start(f32[256,128]{1,0:T(8,128)S(1)} %slice_add_fusion), channel_id=1, source_target_pairs={{0,8},{2,10},{4,12},{6,14},{8,0},{10,2},{12,4},{14,6},{16,24},{18,... | collective-permute-start | bytes 393224 | tf_op jit(solution)/shard_map/ppermute | solution.py:285
  48.2 6.7 %collective-permute-start.23 = (f32[128,128]{1,0:T(8,128)S(1)}, f32[128,128]{1,0:T(8,128)S(1)}, u32[]{:S(2)}, u32[]{:S(2)}) collective-permute-start(f32[128,128]{1,0:T(8,128)S(1)} %fusion.6), channel_id=1, source_target_pairs={{0,16},{2,18},{4,20},{6,22},{8,24},{10,26},{12,28},{14,30},{16,0},... | collective-permute-start | bytes 196616 | tf_op jit(solution)/shard_map/ppermute | solution.py:285
  51.6 5.2 %collective-permute-start.24 = (f32[128,128]{1,0:T(8,128)S(1)}, f32[128,128]{1,0:T(8,128)S(1)}, u32[]{:S(2)}, u32[]{:S(2)}) collective-permute-start(f32[128,128]{1,0:T(8,128)S(1)} %fusion.8), channel_id=1, source_target_pairs={{0,16},{2,18},{4,20},{6,22},{8,24},{10,26},{12,28},{14,30},{16,0},... | collective-permute-start | bytes 196616 | tf_op jit(solution)/shard_map/ppermute | solution.py:285
